TPU v7x, 1024 devices: a whole 8x8x8 slice. The times are simulated.
1024 devices in a mesh: dp: 8 (over y), group: 8 (over x), node: 16 (over z, core).
Axes of the slice: x: 8, y: 8, z: 8, core: 2. Of those that a mesh axis runs over, the one named last changes fastest.
Arguments:
- tokens: bfloat16 [16384, 2048], P(('dp', 'group', 'node')), may hold values from -6 to 6
- cotangent: bfloat16 [16384, 2048], P(('dp', 'group', 'node')), may hold values from -6 to 6
- expert_ids: int32 [16384, 8], P(('dp', 'group', 'node')), may hold values from 0 to 127, as said below
- node_groups: int32 [16384, 4], P(('dp', 'group', 'node')), may hold values from 0 to 7, as said below
- gate_weight: bfloat16 [16384, 8], P(('dp', 'group', 'node')), may hold values from 0.019897461 to 0.29882812
- gate_proj: bfloat16 [128, 2048, 384], P(('group', 'node')), may hold values from -0.125 to 0.125
- up_proj: bfloat16 [128, 2048, 384], P(('group', 'node')), may hold values from -0.125 to 0.125
- down_proj: bfloat16 [128, 384, 2048], P(('group', 'node')), may hold values from -0.3125 to 0.3125
Outputs:
- grad_tokens: bfloat16 [16384, 2048], P(('dp', 'group', 'node'))
- grad_gate_proj: bfloat16 [128, 2048, 384], P(('group', 'node'), 'dp')
- grad_up_proj: bfloat16 [128, 2048, 384], P(('group', 'node'), 'dp')
- grad_down_proj: bfloat16 [128, 384, 2048], P(('group', 'node'), None, 'dp')
Inputs may be any that keep to these rules, and one draw needn't show every extreme that they name: `expert_ids`: each token names 8 distinct experts, 2 of them in each of 4 distinct node groups. Among the tokens of all devices that share a dp index and a node index, no expert is named more than 16 times, and in every such set some expert is named exactly 16 times. `node_groups`: entries of a token's row may repeat; every listed group holds some of the token's named experts, and a named expert outside the listed groups carries no route.
All inputs are finite; a program needn't handle non-finite values.
Results may differ from a plain program's by a relative error of at most 0.017.
Values may be sent and summed in bfloat16 or wider, within the bound.
No kernel may reach another device: no remote copies, remote signals or barrier semaphores. Data moves between devices by JAX's collectives and lax.ppermute only.
A program may use at most 64 MiB of HBM per device.

v0:
```python
import jax
import jax.numpy as jnp
from jax import lax
from jax.sharding import PartitionSpec as P


def expert_pass(routed_rows, cot_rows, gate_matrix, up_matrix, down_matrix):
    contract = (((1,), (1,)), ((), ()))
    gate_value = jnp.dot(routed_rows, gate_matrix, preferred_element_type=jnp.float32)
    up_value = jnp.dot(routed_rows, up_matrix, preferred_element_type=jnp.float32)
    sigmoid_gate = jax.nn.sigmoid(gate_value)
    activated = gate_value * sigmoid_gate
    hidden = (activated * up_value).astype(jnp.bfloat16)
    hidden_grad = lax.dot_general(
        cot_rows, down_matrix, contract, preferred_element_type=jnp.float32
    )
    gate_grad = (
        hidden_grad * up_value * sigmoid_gate * (1.0 + gate_value * (1.0 - sigmoid_gate))
    ).astype(jnp.bfloat16)
    up_grad = (hidden_grad * activated).astype(jnp.bfloat16)
    route_grad = lax.dot_general(
        gate_grad, gate_matrix, contract, preferred_element_type=jnp.float32
    )
    route_grad = route_grad + lax.dot_general(
        up_grad, up_matrix, contract, preferred_element_type=jnp.float32
    )
    return (hidden, gate_grad, up_grad, route_grad.astype(jnp.bfloat16))


def over_rows(left, right):
    return lax.dot_general(
        left, right, (((0,), (0,)), ((), ())), preferred_element_type=jnp.float32
    )


def shards(tokens, cotangent, expert_ids, node_groups, gate_weight, gate_proj, up_proj, down_proj):
    group_count = lax.axis_size("group")
    node_count = lax.axis_size("node")
    tok_count, model_width = tokens.shape
    route_count = expert_ids.shape[1]
    limit_count = node_groups.shape[1]
    per_group = route_count // limit_count
    family = group_count * tok_count
    capacity = (per_group * family + node_count - 1) // node_count
    expert_range = jnp.arange(group_count * node_count, dtype=jnp.int32)
    hits = expert_ids[:, :, None] == expert_range[None, None, :]
    gate_table = jnp.sum(jnp.where(hits, gate_weight[:, :, None].astype(jnp.float32), 0.0), axis=1)
    group_range = jnp.arange(group_count, dtype=jnp.int32)
    picked = jnp.any(node_groups[:, :, None] == group_range[None, None, :], axis=1)
    gate_table = gate_table.reshape(tok_count, group_count, node_count) * picked[:, :, None]
    table_sent = jnp.transpose(gate_table, (1, 0, 2)).astype(jnp.bfloat16)
    keep_mask = jnp.transpose(picked)[:, :, None]
    tokens_sent = jnp.where(keep_mask, tokens[None], jnp.zeros((), tokens.dtype))
    cot_sent = jnp.where(keep_mask, cotangent[None], jnp.zeros((), cotangent.dtype))
    tokens_in, cot_in, table_in = (
        lax.all_to_all(tokens_sent, "group", split_axis=0, concat_axis=0, tiled=True),
        lax.all_to_all(cot_sent, "group", split_axis=0, concat_axis=0, tiled=True),
        lax.all_to_all(table_sent, "group", split_axis=0, concat_axis=0, tiled=True),
    )
    flat_tokens = tokens_in.reshape(family, model_width)
    flat_cot = cot_in.reshape(family, model_width)
    flat_table = table_in.reshape(family, node_count).astype(jnp.float32)
    routed = (flat_table > 0).astype(jnp.int32)
    position = jnp.cumsum(routed, axis=0) - routed
    slot_index = jnp.arange(capacity, dtype=jnp.int32)
    select = (routed[:, :, None] > 0) & (position[:, :, None] == slot_index[None, None, :])
    select = jnp.transpose(select, (1, 2, 0)).astype(jnp.bfloat16)
    slot_tokens = jnp.einsum(
        "ncf,fd->ncd", select, flat_tokens, preferred_element_type=jnp.float32
    ).astype(jnp.bfloat16)
    slot_dy = jnp.einsum(
        "ncf,fd->ncd", select, flat_cot, preferred_element_type=jnp.float32
    ).astype(jnp.bfloat16)
    slot_gate = jnp.einsum("ncf,fn->nc", select.astype(jnp.float32), flat_table)
    slot_cot = (slot_gate[:, :, None] * slot_dy.astype(jnp.float32)).astype(jnp.bfloat16)
    arrived_tokens, arrived_cot = (
        lax.all_to_all(slot_tokens, "node", split_axis=0, concat_axis=0, tiled=True),
        lax.all_to_all(slot_cot, "node", split_axis=0, concat_axis=0, tiled=True),
    )
    routed_rows = arrived_tokens.reshape(-1, model_width)
    cot_rows = arrived_cot.reshape(-1, model_width)
    hidden, gate_grad, up_grad, route_grad = expert_pass(
        routed_rows, cot_rows, gate_proj[0], up_proj[0], down_proj[0]
    )
    returned = lax.all_to_all(
        route_grad.reshape(node_count, capacity, model_width),
        "node",
        split_axis=0,
        concat_axis=0,
        tiled=True,
    )
    group_grad = jnp.einsum(
        "ncf,ncd->fd", select, returned, preferred_element_type=jnp.float32
    ).astype(jnp.bfloat16)
    arrived_home = lax.all_to_all(
        group_grad.reshape(group_count, tok_count, model_width),
        "group",
        split_axis=0,
        concat_axis=0,
        tiled=True,
    )
    grad_tokens = jnp.sum(arrived_home.astype(jnp.float32), axis=0).astype(jnp.bfloat16)
    part_gate = over_rows(routed_rows, gate_grad)
    part_up = over_rows(routed_rows, up_grad)
    part_down = over_rows(hidden, cot_rows)
    sum_gate, sum_up, sum_down = (
        lax.psum_scatter(
            part_gate.astype(jnp.bfloat16), "dp", scatter_dimension=0, tiled=True
        ).astype(jnp.float32),
        lax.psum_scatter(
            part_up.astype(jnp.bfloat16), "dp", scatter_dimension=0, tiled=True
        ).astype(jnp.float32),
        lax.psum_scatter(
            part_down.astype(jnp.bfloat16), "dp", scatter_dimension=1, tiled=True
        ).astype(jnp.float32),
    )
    return (
        grad_tokens,
        sum_gate.astype(jnp.bfloat16)[None],
        sum_up.astype(jnp.bfloat16)[None],
        sum_down.astype(jnp.bfloat16)[None],
    )


def solution(mesh):
    placed = (
        P(("dp", "group", "node"), None),
        P(("dp", "group", "node"), None),
        P(("dp", "group", "node"), None),
        P(("dp", "group", "node"), None),
        P(("dp", "group", "node"), None),
        P(("group", "node"), None, None),
        P(("group", "node"), None, None),
        P(("group", "node"), None, None),
    )
    return jax.shard_map(
        shards,
        mesh=mesh,
        in_specs=placed,
        out_specs=(
            P(("dp", "group", "node"), None),
            P(("group", "node"), "dp", None),
            P(("group", "node"), "dp", None),
            P(("group", "node"), None, "dp"),
        ),
        check_vma=False,
    )
```

profile of v0, /device:TPU:1, one launch (start us, length us, event | category | flops | bytes accessed | tf_op | source)
XLA Modules:
  0.0 283.9 jit_solution(111686980299658952)
XLA Ops:
  7.2 0.8 fusion.24
  8.1 0.8 copy.40
  8.8 0.8 copy.41
  9.9 0.7 reshape.82
  10.6 7.3 %all-to-all-start = ((bf16[8,2,128]{2,1,0:T(2,128)(2,1)}), bf16[8,2,128]{2,1,0:T(2,128)(2,1)S(1)}, u32[]{:S(2)}, u32[]{:S(2)}) async-start(bf16[8,2,128]{2,1,0:T(2,128)(2,1)} %reshape.82), calls=%async_computation | async-start | bytes 8192 | tf_op jit(solution)/shard_map/all_to_all | solution.py:58
  17.9 2.0 broadcast_select_fusion.1
  19.9 4.5 %all-to-all-done = bf16[8,2,128]{2,1,0:T(2,128)(2,1)S(1)} async-done(((bf16[8,2,128]{2,1,0:T(2,128)(2,1)}), bf16[8,2,128]{2,1,0:T(2,128)(2,1)S(1)}, u32[]{:S(2)}, u32[]{:S(2)}) %all-to-all-start) | async-done | bytes 4128 | tf_op jit(solution)/shard_map/all_to_all | solution.py:58
  24.3 3.5 %all-to-all-start.3 = ((bf16[8,16,2048]{2,1,0:T(8,128)(2,1)}), bf16[8,16,2048]{2,1,0:T(8,128)(2,1)S(1)}, u32[]{:S(2)}, u32[]{:S(2)}) async-start(bf16[8,16,2048]{2,1,0:T(8,128)(2,1)} %get-tuple-element.9), calls=%async_computation.3 | async-start | bytes 1048576 | tf_op jit(solution)/shard_map/all_to_all | solution.py:56
  27.9 12.0 %all-to-all-done.3 = bf16[8,16,2048]{2,1,0:T(8,128)(2,1)S(1)} async-done(((bf16[8,16,2048]{2,1,0:T(8,128)(2,1)}), bf16[8,16,2048]{2,1,0:T(8,128)(2,1)S(1)}, u32[]{:S(2)}, u32[]{:S(2)}) %all-to-all-start.3) | async-done | bytes 524320 | tf_op jit(solution)/shard_map/all_to_all | solution.py:56
  39.9 3.5 %all-to-all-start.1 = ((bf16[8,16,2048]{2,1,0:T(8,128)(2,1)}), bf16[8,16,2048]{2,1,0:T(8,128)(2,1)S(1)}, u32[]{:S(2)}, u32[]{:S(2)}) async-start(bf16[8,16,2048]{2,1,0:T(8,128)(2,1)} %get-tuple-element.8), calls=%async_computation.1 | async-start | bytes 1048576 | tf_op jit(solution)/shard_map/all_to_all | solution.py:57
  43.8 1.5 convolution_convert_fusion.3
  45.3 12.6 %all-to-all-done.1 = bf16[8,16,2048]{2,1,0:T(8,128)(2,1)S(1)} async-done(((bf16[8,16,2048]{2,1,0:T(8,128)(2,1)}), bf16[8,16,2048]{2,1,0:T(8,128)(2,1)S(1)}, u32[]{:S(2)}, u32[]{:S(2)}) %all-to-all-start.1) | async-done | bytes 524320 | tf_op jit(solution)/shard_map/all_to_all | solution.py:57
  57.9 24.1 %all-to-all-start.4 = ((bf16[16,16,2048]{2,1,0:T(8,128)(2,1)}), bf16[16,16,2048]{2,1,0:T(8,128)(2,1)S(1)}, u32[]{:S(2)}, u32[]{:S(2)}) async-start(bf16[16,16,2048]{2,1,0:T(8,128)(2,1)} %convolution_convert_fusion.3), calls=%async_computation.4 | async-start | bytes 2097152 | tf_op jit(solution)/shard_map/all_to_all | solution.py:77
  82.2 1.4 fusion.2
  83.6 26.3 %all-to-all-done.4 = bf16[16,16,2048]{2,1,0:T(8,128)(2,1)S(1)} async-done(((bf16[16,16,2048]{2,1,0:T(8,128)(2,1)}), bf16[16,16,2048]{2,1,0:T(8,128)(2,1)S(1)}, u32[]{:S(2)}, u32[]{:S(2)}) %all-to-all-start.4) | async-done | bytes 1048608 | tf_op jit(solution)/shard_map/all_to_all | solution.py:77
  109.9 4.2 %all-to-all-start.2 = ((bf16[16,16,2048]{2,1,0:T(8,128)(2,1)}), bf16[16,16,2048]{2,1,0:T(8,128)(2,1)}, u32[]{:S(2)}, u32[]{:S(2)}) async-start(bf16[16,16,2048]{2,1,0:T(8,128)(2,1)} %fusion.2), calls=%async_computation.2 | async-start | bytes 2097152 | tf_op jit(solution)/shard_map/all_to_all | solution.py:78
  114.2 0.7 fusion.7
  115.6 1.5 fusion.10
  117.1 24.4 %all-to-all-done.2 = bf16[16,16,2048]{2,1,0:T(8,128)(2,1)} async-done(((bf16[16,16,2048]{2,1,0:T(8,128)(2,1)}), bf16[16,16,2048]{2,1,0:T(8,128)(2,1)}, u32[]{:S(2)}, u32[]{:S(2)}) %all-to-all-start.2) | async-done | bytes 1048608 | tf_op jit(solution)/shard_map/all_to_all | solution.py:78
  141.4 3.1 %convolution_convert_fusion = bf16[384,2048]{1,0:T(8,128)(2,1)} fusion(bf16[256,2048]{1,0:T(8,128)(2,1)} %bitcast.10, f32[256,384]{1,0:T(8,128)} %fusion.10, f32[256,384]{1,0:T(8,128)S(1)} %fusion.7), kind=kOutput, calls=%fused_computation | convolution fusion | flops 404029440 | bytes 3407872 | tf_op jit(solution)/shard_map/dot_general | solution.py:31
  144.7 2.6 multiply_convert_fusion.1
  147.2 1.9 convolution_convert_fusion.1
  149.2 0.7 fusion.5
  150.6 1.8 fusion.3
  152.3 4.2 %all-to-all-start.5 = ((bf16[16,16,2048]{2,1,0:T(8,128)(2,1)}), bf16[16,16,2048]{2,1,0:T(8,128)(2,1)}, u32[]{:S(2)}, u32[]{:S(2)}) async-start(bf16[16,16,2048]{2,1,0:T(8,128)(2,1)} %bitcast.66), calls=%async_computation.5 | async-start | bytes 2097152 | tf_op jit(solution)/shard_map/all_to_all | solution.py:85
  156.6 1.9 convolution_convert_fusion.2
  158.6 25.3 %all-to-all-done.5 = bf16[16,16,2048]{2,1,0:T(8,128)(2,1)} async-done(((bf16[16,16,2048]{2,1,0:T(8,128)(2,1)}), bf16[16,16,2048]{2,1,0:T(8,128)(2,1)}, u32[]{:S(2)}, u32[]{:S(2)}) %all-to-all-start.5) | async-done | bytes 1048608 | tf_op jit(solution)/shard_map/all_to_all | solution.py:85
  183.9 2.0 fusion.4
  185.9 19.5 %all_to_all.35 = bf16[8,16,2048]{2,1,0:T(8,128)(2,1)S(1)} all-to-all(bf16[8,16,2048]{2,1,0:T(8,128)(2,1)S(1)} %bitcast.69), channel_id=1, replica_groups=mesh['dp'=8,'group'=8,'node'=16] {'group'}, dimensions={0} | all-to-all | bytes 1048576 | tf_op jit(solution)/shard_map/all_to_all | solution.py:95
  205.3 0.7 reduce_sum.22
  206.0 22.4 %reduce-scatter.6.cloned.1.call-done = bf16[256,384]{1,0:T(8,128)(2,1)} async-done(((bf16[2048,384]{1,0:T(8,128)(2,1)}), bf16[256,384]{1,0:T(8,128)(2,1)}) %reduce-scatter.6.cloned.1.call-update) | async-done | bytes 196624 | tf_op jit(solution)/shard_map/reduce_scatter | solution.py:110
  228.5 48.9 %reduce-scatter.4.cloned.1.call-done = bf16[256,384]{1,0:T(8,128)(2,1)} async-done(((bf16[2048,384]{1,0:T(8,128)(2,1)}), bf16[256,384]{1,0:T(8,128)(2,1)}) %reduce-scatter.4.cloned.1.call-update) | async-done | bytes 196624 | tf_op jit(solution)/shard_map/reduce_scatter | solution.py:107
  (28 shorter events, 2.6 us)
Async XLA Ops:
  7.2 107.0 %copy-start = (bf16[1,2048,384]{2,1,0:T(8,128)(2,1)S(1)}, bf16[1,2048,384]{2,1,0:T(8,128)(2,1)}, u32[]{:S(2)}) copy-start(bf16[1,2048,384]{2,1,0:T(8,128)(2,1)} %param.13) | copy-start | bytes 4718596
  10.6 13.8 %all-to-all-start = ((bf16[8,2,128]{2,1,0:T(2,128)(2,1)}), bf16[8,2,128]{2,1,0:T(2,128)(2,1)S(1)}, u32[]{:S(2)}, u32[]{:S(2)}) async-start(bf16[8,2,128]{2,1,0:T(2,128)(2,1)} %reshape.82), calls=%async_computation | async-start | bytes 8192 | tf_op jit(solution)/shard_map/all_to_all | solution.py:58
  24.3 15.6 %all-to-all-start.3 = ((bf16[8,16,2048]{2,1,0:T(8,128)(2,1)}), bf16[8,16,2048]{2,1,0:T(8,128)(2,1)S(1)}, u32[]{:S(2)}, u32[]{:S(2)}) async-start(bf16[8,16,2048]{2,1,0:T(8,128)(2,1)} %get-tuple-element.9), calls=%async_computation.3 | async-start | bytes 1048576 | tf_op jit(solution)/shard_map/all_to_all | solution.py:56
  39.9 17.9 %all-to-all-start.1 = ((bf16[8,16,2048]{2,1,0:T(8,128)(2,1)}), bf16[8,16,2048]{2,1,0:T(8,128)(2,1)S(1)}, u32[]{:S(2)}, u32[]{:S(2)}) async-start(bf16[8,16,2048]{2,1,0:T(8,128)(2,1)} %get-tuple-element.8), calls=%async_computation.1 | async-start | bytes 1048576 | tf_op jit(solution)/shard_map/all_to_all | solution.py:57
  57.9 52.0 %all-to-all-start.4 = ((bf16[16,16,2048]{2,1,0:T(8,128)(2,1)}), bf16[16,16,2048]{2,1,0:T(8,128)(2,1)S(1)}, u32[]{:S(2)}, u32[]{:S(2)}) async-start(bf16[16,16,2048]{2,1,0:T(8,128)(2,1)} %convolution_convert_fusion.3), calls=%async_computation.4 | async-start | bytes 2097152 | tf_op jit(solution)/shard_map/all_to_all | solution.py:77
  109.9 31.6 %all-to-all-start.2 = ((bf16[16,16,2048]{2,1,0:T(8,128)(2,1)}), bf16[16,16,2048]{2,1,0:T(8,128)(2,1)}, u32[]{:S(2)}, u32[]{:S(2)}) async-start(bf16[16,16,2048]{2,1,0:T(8,128)(2,1)} %fusion.2), calls=%async_computation.2 | async-start | bytes 2097152 | tf_op jit(solution)/shard_map/all_to_all | solution.py:78
  114.1 91.9 %reduce-scatter.8.cloned.1.call-start = ((), (), s32[]{:S(2)}) async-start(), calls=%async_computation.12 | async-start | bytes 1769472 | tf_op jit(solution)/shard_map/reduce_scatter | solution.py:113
  114.2 1.4 copy-start.1
  144.6 83.8 %reduce-scatter.6.cloned.1.call-start = ((), (), s32[]{:S(2)}) async-start(), calls=%async_computation.11 | async-start | bytes 1769472 | tf_op jit(solution)/shard_map/reduce_scatter | solution.py:110
  149.1 1.4 copy-start.2
  152.3 31.6 %all-to-all-start.5 = ((bf16[16,16,2048]{2,1,0:T(8,128)(2,1)}), bf16[16,16,2048]{2,1,0:T(8,128)(2,1)}, u32[]{:S(2)}, u32[]{:S(2)}) async-start(bf16[16,16,2048]{2,1,0:T(8,128)(2,1)} %bitcast.66), calls=%async_computation.5 | async-start | bytes 2097152 | tf_op jit(solution)/shard_map/all_to_all | solution.py:85
  156.6 120.8 %reduce-scatter.4.cloned.1.call-start = ((), (), s32[]{:S(2)}) async-start(), calls=%async_computation.10 | async-start | bytes 1769472 | tf_op jit(solution)/shard_map/reduce_scatter | solution.py:107
Sparse Core Ops, SparseCore 0:
  144.7 34.6 reduce-scatter.7
  183.5 44.9 reduce-scatter.5
  232.5 44.8 reduce-scatter.3
where the time goes:
time: 287 us; the launch traced here: 284 us
  waiting for transfers between devices  176 us (61%)
  starting transfers between devices  47 us (16%)
  blocking collectives  19.5 us (7%)
  matrix products  19.2 us (7%)
  between operations  13.9 us (5%)
  local copies, waits for them, and re-layouts  3.97 us (1%)
  other arithmetic  3.96 us (1%)
    reduce_scatter x1, waiting for transfers between devices, shards(): lax.psum_scatter(part_gate.astype(jnp.bfloat16), 'dp', scatter_dimension=...  48.9 us
    all_to_all x1, waiting for transfers between devices, shards(): lax.all_to_all(slot_tokens, 'node', split_axis=0, concat_axis=0, tiled=True)  26.3 us
    all_to_all x1, waiting for transfers between devices, shards(): lax.all_to_all(route_grad.reshape(node_count, capacity, model_width), 'no...  25.3 us
    all_to_all x1, waiting for transfers between devices, shards(): lax.all_to_all(slot_cot, 'node', split_axis=0, concat_axis=0, tiled=True)  24.4 us
    all_to_all x1, starting transfers between devices, shards(): lax.all_to_all(slot_tokens, 'node', split_axis=0, concat_axis=0, tiled=True)  24.1 us
    reduce_scatter x1, waiting for transfers between devices, shards(): lax.psum_scatter(part_up.astype(jnp.bfloat16), 'dp', scatter_dimension=0,...  22.4 us
    all_to_all x1, blocking collectives, shards(): lax.all_to_all(group_grad.reshape(group_count, tok_count, model_width), '...  19.5 us
    all_to_all x1, waiting for transfers between devices, shards(): lax.all_to_all(cot_sent, 'group', split_axis=0, concat_axis=0, tiled=True)  12.6 us
  transfers between devices with their start and end apart: 9, of which 8 were waited for; matrix products, arithmetic and copies ran while one was open for 7% of the time, Pallas kernels for 0%

commit v1 on v0

v1 whole, which is shorter than its diff:
```python
import functools

import jax
import jax.numpy as jnp
from jax import lax
from jax.experimental import pallas as pl
from jax.experimental.pallas import tpu as pltpu
from jax.sharding import PartitionSpec as P

F32 = jnp.float32
BF16 = jnp.bfloat16
LANES = 128


def contract(left, right, left_dim, right_dim):
    return lax.dot_general(
        left, right, (((left_dim,), (right_dim,)), ((), ())), preferred_element_type=F32
    )


def add(left, right):
    return (left.astype(F32) + right.astype(F32)).astype(BF16)


def to_owners(partial, returned, send_home):
    count, rows, _ = partial.shape
    nodes = lax.axis_size("node")
    half, reach = rows // 2, count // 2
    me = lax.axis_index("dp")
    first = jnp.where((me + lax.axis_index("node")) % 2 == 0, 1, -1)

    def exchange(block, flip):
        pairs = []
        for i in range(count):
            for n in range(nodes):
                step = 1 if (i + n + flip) % 2 == 0 else -1
                pairs.append((i * nodes + n, (i + step) % count * nodes + n))
        return lax.ppermute(block, ("dp", "node"), pairs)

    def own(offset):
        return lax.dynamic_index_in_dim(partial, (me + offset + count) % count, 0, keepdims=False)

    farthest = own(reach)
    turn, home = 0, None
    arrived = [exchange(farthest[:half], 0), exchange(farthest[half:], 1)]
    for hop in range(reach - 1, 0, -1):
        turn = 1 - turn
        toward = first if turn == 0 else -first
        blocks = [own(toward * hop), own(-toward * hop)]
        if hop == reach - 1:
            blocks = [
                jnp.concatenate([add(blocks[0][:half], arrived[0]), blocks[0][half:]], axis=0),
                jnp.concatenate([blocks[1][:half], add(blocks[1][half:], arrived[1])], axis=0),
            ]
        else:
            blocks = [add(mine, sent) for mine, sent in zip(blocks, arrived)]
        if hop == reach - 2:
            blocks, returned = lax.optimization_barrier((blocks, returned))
            home = send_home(returned)
        if hop == reach - 3:
            blocks, home = lax.optimization_barrier((blocks, home))
        arrived = [exchange(blocks[0], turn), exchange(blocks[1], 1 - turn)]
    total = own(0).astype(F32) + arrived[0].astype(F32) + arrived[1].astype(F32)
    return total.astype(BF16), home


def send_kernel(node_count, tokens, cotangent, expert_ids, node_groups, gate_weight, sent):
    group_count, tok_count, _ = sent.shape
    width = tokens.shape[1]
    choices, limit = expert_ids.shape[0], node_groups.shape[0]
    weights = gate_weight[...].astype(F32)
    expert = lax.broadcasted_iota(jnp.int32, (group_count * node_count, tok_count), 0)
    table = jnp.zeros(expert.shape, F32)
    for k in range(choices):
        table = table + jnp.where(expert_ids[k : k + 1, :] == expert, weights[k : k + 1, :], 0.0)
    for g in range(group_count):
        picked = node_groups[0:1, :] == g
        for j in range(1, limit):
            picked = picked | (node_groups[j : j + 1, :] == g)
        block = jnp.where(picked, table[g * node_count : (g + 1) * node_count, :], 0.0)
        sent[g, :, :width] = tokens[...]
        sent[g, :, width : 2 * width] = cotangent[...]
        sent[g, :, 2 * width :] = jnp.zeros((tok_count, LANES), BF16)
        sent[g, :node_count, 2 * width : 2 * width + tok_count] = block.astype(BF16)


def slot_kernel(arrived, slots, select):
    group_count, tok_count, _ = arrived.shape
    node_count, capacity, width = slots.shape
    width = width // 2
    family = group_count * tok_count
    table = [arrived[g, :node_count, 2 * width : 2 * width + tok_count] for g in range(group_count)]
    table = jnp.concatenate([part.astype(F32) for part in table], axis=1)
    routed = table > 0
    row = lax.broadcasted_iota(jnp.int32, (family, family), 0)
    column = lax.broadcasted_iota(jnp.int32, (family, family), 1)
    earlier = jnp.where(row < column, 1.0, 0.0).astype(BF16)
    position = contract(jnp.where(routed, 1.0, 0.0).astype(BF16), earlier, 1, 0)
    place = jnp.where(routed, position, -1.0)[:, None, :]
    slot = lax.broadcasted_iota(jnp.int32, (node_count, capacity, family), 1).astype(F32)
    taken = place == slot
    picks = jnp.where(taken, 1.0, 0.0).reshape(node_count * capacity, family).astype(BF16)
    weighted = jnp.where(taken, table[:, None, :], 0.0).reshape(node_count * capacity, family).astype(BF16)
    select[...] = picks
    cut = width // 4
    for start in range(0, 2 * width, cut):
        part = slice(start, start + cut)
        block = arrived[:, :, part].reshape(family, cut)
        out = contract(picks if start < width else weighted, block, 1, 0)
        slots[:, :, part] = out.reshape(node_count, capacity, cut).astype(BF16)


def expert_kernel(
    landed, gate_hbm, up_hbm, down_hbm, hidden, pair_grad, route_grad, gate_proj, up_proj, down_proj, done
):
    width, hid = gate_proj.shape
    loads = [
        pltpu.make_async_copy(gate_hbm, gate_proj, done.at[0]),
        pltpu.make_async_copy(up_hbm, up_proj, done.at[1]),
        pltpu.make_async_copy(down_hbm, down_proj, done.at[2]),
    ]
    for load in loads:
        load.start()
    loads[0].wait()
    gate_value = contract(landed[:, :width], gate_proj[...], 1, 0)
    loads[1].wait()
    up_value = contract(landed[:, :width], up_proj[...], 1, 0)
    sigmoid = 1.0 / (1.0 + jnp.exp(-gate_value))
    silu = gate_value * sigmoid
    hidden[...] = (silu * up_value).astype(BF16)
    loads[2].wait()
    hidden_grad = contract(landed[:, width:], down_proj[...], 1, 1)
    slope = up_value * sigmoid * (1.0 + gate_value * (1.0 - sigmoid))
    pair_grad[:, :hid] = (hidden_grad * slope).astype(BF16)
    pair_grad[:, hid:] = (hidden_grad * silu).astype(BF16)
    cut = width // 4
    for start in range(0, width, cut):
        part = slice(start, start + cut)
        grad = contract(pair_grad[:, :hid], gate_proj[part, :], 1, 1)
        grad = grad + contract(pair_grad[:, hid:], up_proj[part, :], 1, 1)
        route_grad[:, part] = grad.astype(BF16)


def weights_kernel(landed, pair_grad, hidden, partial):
    count, cut, _ = partial.shape
    pair = pair_grad.shape[1]
    width = count * cut
    for block in range(count):
        rows = landed[:, block * cut : (block + 1) * cut]
        cot_rows = landed[:, width + block * cut : width + (block + 1) * cut]
        partial[block, :, :pair] = contract(rows, pair_grad[...], 0, 0).astype(BF16)
        partial[block, :, pair:] = contract(cot_rows, hidden[...], 0, 0).astype(BF16)


def run(kernel, out, *args, flops=0, **kwargs):
    held = sum(x.size * x.dtype.itemsize for x in (*args, *out))
    return pl.pallas_call(
        kernel,
        out_shape=out,
        cost_estimate=pl.CostEstimate(flops=flops, bytes_accessed=held, transcendentals=0),
        compiler_params=pltpu.CompilerParams(vmem_limit_bytes=40 * 1024 * 1024),
        **kwargs,
    )(*args)


def shards(tokens, cotangent, expert_ids, node_groups, gate_weight, gate_proj, up_proj, down_proj):
    data_count = lax.axis_size("dp")
    group_count = lax.axis_size("group")
    node_count = lax.axis_size("node")
    tok_count, width = tokens.shape
    hid = down_proj.shape[1]
    per_group = expert_ids.shape[1] // node_groups.shape[1]
    family = group_count * tok_count
    capacity = (per_group * family + node_count - 1) // node_count
    count = node_count * capacity
    dot_flops = 2 * count * width * hid

    def shape(*dims):
        return jax.ShapeDtypeStruct(dims, BF16)

    def over(axis, blocks):
        return lax.all_to_all(blocks, axis, split_axis=0, concat_axis=0, tiled=True)

    (sent,) = run(
        functools.partial(send_kernel, node_count),
        (shape(group_count, tok_count, 2 * width + LANES),),
        tokens, cotangent, expert_ids.T, node_groups.T, gate_weight.T,
    )
    arrived = over("group", sent)
    slots, select = run(
        slot_kernel,
        (shape(node_count, capacity, 2 * width), shape(count, family)),
        arrived,
        flops=4 * count * family * width,
    )
    landed = over("node", slots).reshape(count, 2 * width)
    whole = pl.BlockSpec(memory_space=pltpu.VMEM)
    far = pl.BlockSpec(memory_space=pl.ANY)
    hidden, pair_grad, route_grad = run(
        expert_kernel,
        (shape(count, hid), shape(count, 2 * hid), shape(count, width)),
        landed, gate_proj[0], up_proj[0], down_proj[0],
        flops=5 * dot_flops,
        in_specs=[whole, far, far, far],
        out_specs=[whole] * 3,
        scratch_shapes=[
            pltpu.VMEM((width, hid), BF16),
            pltpu.VMEM((width, hid), BF16),
            pltpu.VMEM((hid, width), BF16),
            pltpu.SemaphoreType.DMA((3,)),
        ],
    )
    pair_grad, route_grad = lax.optimization_barrier((pair_grad, route_grad))
    returned = over("node", route_grad.reshape(node_count, capacity, width))

    def send_home(returned):
        group_grad = contract(select, returned.reshape(count, width), 0, 0).astype(BF16)
        return over("group", group_grad.reshape(group_count, tok_count, width))

    (partial,) = run(
        weights_kernel,
        (shape(data_count, width // data_count, 3 * hid),),
        landed, pair_grad, hidden,
        flops=3 * dot_flops,
    )
    total, home = to_owners(partial, returned, send_home)
    grad_tokens = jnp.sum(home.astype(F32), axis=0).astype(BF16)
    return (
        grad_tokens,
        total[None, :, :hid],
        total[None, :, hid : 2 * hid],
        total[:, 2 * hid :].T[None],
    )


def solution(mesh):
    rows = P(("dp", "group", "node"), None)
    experts = P(("group", "node"), None, None)
    return jax.shard_map(
        shards,
        mesh=mesh,
        in_specs=(rows,) * 5 + (experts,) * 3,
        out_specs=(
            rows,
            P(("group", "node"), "dp", None),
            P(("group", "node"), "dp", None),
            P(("group", "node"), None, "dp"),
        ),
        check_vma=False,
    )
```

time: 287 us -> 215 us (0.75)
  waiting for transfers between devices: 176 us -> 94.3 us
  matrix products: 19.2 us -> 1.15 us
  starting transfers between devices: 47 us -> 62.1 us
  between operations: 13.9 us -> 0.88 us
  local copies, waits for them, and re-layouts: 3.97 us -> 13.2 us
  Pallas kernels: 0 us -> 7.25 us
  blocking collectives: 19.5 us -> 26.4 us
  other arithmetic: 3.96 us -> 8.46 us
    reduce_scatter x3 -> x0, waiting for transfers between devices: 71.3 us -> none  [the longest x1 48.9 us: shards(): lax.psum_scatter(part_gate.astype(jnp.bfloat16), 'dp', scatter_dimension=...]
    all_to_all x6 -> x3, waiting for transfers between devices: 105 us -> 62.5 us  [over(): return lax.all_to_all(blocks, axis, split_axis=0, concat_axis=0, tiled=True)]
    ppermute x0 -> x8, waiting for transfers between devices: none -> 31.8 us  [exchange(): return lax.ppermute(block, ('dp', 'node'), pairs)]
    ppermute x0 -> x8, starting transfers between devices: none -> 26.1 us  [exchange(): return lax.ppermute(block, ('dp', 'node'), pairs)]
    dot_general x12 -> x1, matrix products: 19.2 us -> 1.15 us  [contract(): lax.dot_general(left, right, (((left_dim,), (right_dim,)), ((), ())), pre...]
    all_to_all x6 -> x3, starting transfers between devices: 46.8 us -> 36 us  [over(): return lax.all_to_all(blocks, axis, split_axis=0, concat_axis=0, tiled=True)]
    unnamed x9 -> x21, local copies, waits for them, and re-layouts: 2.88 us -> 12.2 us
    pallas_call x0 -> x4, Pallas kernels: none -> 7.25 us  [run(): pl.pallas_call(kernel, out_shape=out, cost_estimate=pl.CostEstimate(flops...]
  transfers between devices with their start and end apart: 9 -> 11, of which waited for: 8 -> 10; matrix products, arithmetic and copies ran while one was open for 7% -> 4% of each run, Pallas kernels for 0% -> 0%
where the time goes in v1:
time: 215 us; the launch traced here: 214 us
  waiting for transfers between devices  94.3 us (44%)
  starting transfers between devices  62.1 us (29%)
  blocking collectives  26.4 us (12%)
  local copies, waits for them, and re-layouts  13.2 us (6%)
  other arithmetic  8.46 us (4%)
  Pallas kernels  7.25 us (3%)
    all_to_all x3, waiting for transfers between devices, over(): return lax.all_to_all(blocks, axis, split_axis=0, concat_axis=0, tiled=True)  62.5 us
    all_to_all x3, starting transfers between devices, over(): return lax.all_to_all(blocks, axis, split_axis=0, concat_axis=0, tiled=True)  36 us
    ppermute x8, waiting for transfers between devices, exchange(): return lax.ppermute(block, ('dp', 'node'), pairs)  31.8 us
    all_to_all x1, blocking collectives, over(): return lax.all_to_all(blocks, axis, split_axis=0, concat_axis=0, tiled=True)  26.4 us
    ppermute x8, starting transfers between devices, exchange(): return lax.ppermute(block, ('dp', 'node'), pairs)  26.1 us
    unnamed x21, local copies, waits for them, and re-layouts  12.2 us
    pallas_call x4, Pallas kernels, run(): pl.pallas_call(kernel, out_shape=out, cost_estimate=pl.CostEstimate(flops...  7.25 us
    convert_element_type x3, other arithmetic, add(): return (left.astype(F32) + right.astype(F32)).astype(BF16)  5.58 us
  transfers between devices with their start and end apart: 11, of which 10 were waited for; matrix products, arithmetic and copies ran while one was open for 4% of the time, Pallas kernels for 0%

profile of v1, /device:TPU:1, one launch (start us, length us, event | category | flops | bytes accessed | tf_op | source)
XLA Modules:
  0.0 213.7 jit_solution(3989695655138699221)
XLA Ops:
  4.5 26.4 %all_to_all.20.arrived = bf16[8,16,4224]{2,1,0:T(8,128)(2,1)S(1)} all-to-all(bf16[8,16,4224]{2,1,0:T(8,128)(2,1)S(1)} %shard_map.111), channel_id=1, replica_groups=mesh['dp'=8,'group'=8,'node'=16] {'group'}, dimensions={0} | all-to-all | bytes 2162688 | tf_op jit(solution)/shard_map/all_to_all | solution.py:182
  31.8 1.3 copy-done.1
  33.1 27.8 %all-to-all-start.1 = ((bf16[16,16,4096]{2,1,0:T(8,128)(2,1)}), bf16[16,16,4096]{2,1,0:T(8,128)(2,1)S(1)}, u32[]{:S(2)}, u32[]{:S(2)}) async-start(bf16[16,16,4096]{2,1,0:T(8,128)(2,1)} %copy-done.1), calls=%async_computation.1 | async-start | bytes 4194304 | tf_op jit(solution)/shard_map/all_to_all | solution.py:182
  60.9 49.0 %all-to-all-done.1 = bf16[16,16,4096]{2,1,0:T(8,128)(2,1)S(1)} async-done(((bf16[16,16,4096]{2,1,0:T(8,128)(2,1)}), bf16[16,16,4096]{2,1,0:T(8,128)(2,1)S(1)}, u32[]{:S(2)}, u32[]{:S(2)}) %all-to-all-start.1) | async-done | bytes 2097184 | tf_op jit(solution)/shard_map/all_to_all | solution.py:182
  109.9 1.4 copy-done.7
  111.3 1.4 copy-done.8
  112.7 1.4 copy-done.9
  114.1 4.7 %shard_map.113 = (bf16[256,384]{1,0:T(8,128)(2,1)S(1)}, bf16[256,768]{1,0:T(8,128)(2,1)S(1)}, bf16[256,2048]{1,0:T(8,128)(2,1)}) custom-call(bf16[256,4096]{1,0:T(8,128)(2,1)S(1)} %bitcast.53, bf16[2048,384]{1,0:T(8,128)(2,1)S(1)} %bitcast.58, bf16[2048,384]{1,0:T(8,128)(2,1)S(1)} %bitcast.59, bf16[384,2048]{1,0:T(8,128)(2,1)S(1)} %bitcast.60), custom_call_target="tpu_custom_call" | custom-call | flops 2013265920 | bytes 8454144 | tf_op jit(solution)/shard_map/pallas_call | solution.py:157
  118.8 1.6 shard_map.114
  120.4 2.1 %copy-done = bf16[8,256,1152]{2,1,0:T(8,128)(2,1)} copy-done((bf16[8,256,1152]{2,1,0:T(8,128)(2,1)}, bf16[8,256,1152]{2,1,0:T(8,128)(2,1)S(1)}, u32[]{:S(2)}) %copy-start) | copy-done | bytes 4718616
  122.6 3.3 %collective-permute-start.2 = (bf16[128,1152]{1,0:T(8,128)(2,1)S(1)}, bf16[128,1152]{1,0:T(8,128)(2,1)S(1)}, u32[]{:S(2)}, u32[]{:S(2)}) collective-permute-start(bf16[128,1152]{1,0:T(8,128)(2,1)S(1)} %get-tuple-element.40), channel_id=1, source_target_pairs={{0,896},{1,129},{2,898},{3,131},{4,900},{5,133},{6,902},{7,135},{8... | collective-permute-start | bytes 884744 | tf_op jit(solution)/shard_map/ppermute | solution.py:38
  125.9 5.5 %collective-permute-start = (bf16[128,1152]{1,0:T(8,128)(2,1)S(1)}, bf16[128,1152]{1,0:T(8,128)(2,1)S(1)}, u32[]{:S(2)}, u32[]{:S(2)}) collective-permute-start(bf16[128,1152]{1,0:T(8,128)(2,1)S(1)} %get-tuple-element.39), channel_id=1, source_target_pairs={{0,128},{1,897},{2,130},{3,899},{4,132},{5,901},{6,134},{7,903},{8... | collective-permute-start | bytes 884744 | tf_op jit(solution)/shard_map/ppermute | solution.py:38
  131.4 4.7 %all-to-all-start.2 = ((bf16[16,16,2048]{2,1,0:T(8,128)(2,1)}), bf16[16,16,2048]{2,1,0:T(8,128)(2,1)S(1)}, u32[]{:S(2)}, u32[]{:S(2)}) async-start(bf16[16,16,2048]{2,1,0:T(8,128)(2,1)} %bitcast.16), calls=%async_computation.2 | async-start | bytes 2097152 | tf_op jit(solution)/shard_map/all_to_all | solution.py:182
  136.3 1.2 fusion.6
  137.6 4.9 %collective-permute-start.3 = (bf16[256,1152]{1,0:T(8,128)(2,1)S(1)}, bf16[256,1152]{1,0:T(8,128)(2,1)}, u32[]{:S(2)}, u32[]{:S(2)}) collective-permute-start(bf16[256,1152]{1,0:T(8,128)(2,1)S(1)} %pad_maximum_fusion.1), channel_id=1, source_target_pairs={{0,128},{1,897},{2,130},{3,899},{4,132},{5,901},{6,134},{7,903},{8... | collective-permute-start | bytes 1769480 | tf_op jit(solution)/shard_map/ppermute | solution.py:38
  143.3 1.9 collective-permute-start.1
  145.2 6.4 %collective-permute-done.3 = bf16[256,1152]{1,0:T(8,128)(2,1)} collective-permute-done((bf16[256,1152]{1,0:T(8,128)(2,1)S(1)}, bf16[256,1152]{1,0:T(8,128)(2,1)}, u32[]{:S(2)}, u32[]{:S(2)}) %collective-permute-start.3) | collective-permute-done | bytes 589856 | tf_op jit(solution)/shard_map/ppermute | solution.py:38
  151.6 5.1 %collective-permute-done.1 = bf16[256,1152]{1,0:T(8,128)(2,1)} collective-permute-done((bf16[256,1152]{1,0:T(8,128)(2,1)}, bf16[256,1152]{1,0:T(8,128)(2,1)}, u32[]{:S(2)}, u32[]{:S(2)}) %collective-permute-start.1) | collective-permute-done | bytes 589856 | tf_op jit(solution)/shard_map/ppermute | solution.py:38
  156.7 1.9 fusion.3
  158.6 5.5 %all-to-all-done.2 = bf16[16,16,2048]{2,1,0:T(8,128)(2,1)S(1)} async-done(((bf16[16,16,2048]{2,1,0:T(8,128)(2,1)}), bf16[16,16,2048]{2,1,0:T(8,128)(2,1)S(1)}, u32[]{:S(2)}, u32[]{:S(2)}) %all-to-all-start.2) | async-done | bytes 1048608 | tf_op jit(solution)/shard_map/all_to_all | solution.py:182
  164.1 3.2 %collective-permute-start.5 = (bf16[256,1152]{1,0:T(8,128)(2,1)S(1)}, bf16[256,1152]{1,0:T(8,128)(2,1)S(1)}, u32[]{:S(2)}, u32[]{:S(2)}) collective-permute-start(bf16[256,1152]{1,0:T(8,128)(2,1)S(1)} %get-tuple-element.24), channel_id=1, source_target_pairs={{0,896},{1,129},{2,898},{3,131},{4,900},{5,133},{6,902},{7,135},{8... | collective-permute-start | bytes 1769480 | tf_op jit(solution)/shard_map/ppermute | solution.py:38
  167.3 2.5 %collective-permute-start.4 = (bf16[256,1152]{1,0:T(8,128)(2,1)S(1)}, bf16[256,1152]{1,0:T(8,128)(2,1)}, u32[]{:S(2)}, u32[]{:S(2)}) collective-permute-start(bf16[256,1152]{1,0:T(8,128)(2,1)S(1)} %get-tuple-element.23), channel_id=1, source_target_pairs={{0,128},{1,897},{2,130},{3,899},{4,132},{5,901},{6,134},{7,903},{8... | collective-permute-start | bytes 1769480 | tf_op jit(solution)/shard_map/ppermute | solution.py:38
  170.9 3.5 %all-to-all-start.3 = ((bf16[8,16,2048]{2,1,0:T(8,128)(2,1)}), bf16[8,16,2048]{2,1,0:T(8,128)(2,1)S(1)}, u32[]{:S(2)}, u32[]{:S(2)}) async-start(bf16[8,16,2048]{2,1,0:T(8,128)(2,1)} %bitcast.19), calls=%async_computation.3 | async-start | bytes 1048576 | tf_op jit(solution)/shard_map/all_to_all | solution.py:182
  174.5 3.6 %collective-permute-done.5 = bf16[256,1152]{1,0:T(8,128)(2,1)S(1)} collective-permute-done((bf16[256,1152]{1,0:T(8,128)(2,1)S(1)}, bf16[256,1152]{1,0:T(8,128)(2,1)S(1)}, u32[]{:S(2)}, u32[]{:S(2)}) %collective-permute-start.5) | collective-permute-done | bytes 589856 | tf_op jit(solution)/shard_map/ppermute | solution.py:38
  178.0 3.7 %collective-permute-done.4 = bf16[256,1152]{1,0:T(8,128)(2,1)} collective-permute-done((bf16[256,1152]{1,0:T(8,128)(2,1)S(1)}, bf16[256,1152]{1,0:T(8,128)(2,1)}, u32[]{:S(2)}, u32[]{:S(2)}) %collective-permute-start.4) | collective-permute-done | bytes 589856 | tf_op jit(solution)/shard_map/ppermute | solution.py:38
  181.8 2.5 %fusion.2 = (bf16[256,1152]{1,0:T(8,128)(2,1)}, bf16[256,1152]{1,0:T(8,128)(2,1)S(1)}) fusion(bf16[256,1152]{1,0:T(8,128)(2,1)S(1)} %collective-permute-done.5, bf16[8,256,1152]{2,1,0:T(8,128)(2,1)} %copy-done, s32[]{:T(128)S(6)} %select_n.83, bf16[256,1152]{1,0:T(8,128)(2,1)} %collective-permute-done.4, s32[]{:T(128)S(6)} %select_n.71), kind=kLoop, calls=%fused_computation.5 | loop fusion | flops 2359296 | bytes 3538952 | tf_op jit(solution)/shard_map/convert_element_type | solution.py:22
  184.3 8.1 %all-to-all-done.3 = bf16[8,16,2048]{2,1,0:T(8,128)(2,1)S(1)} async-done(((bf16[8,16,2048]{2,1,0:T(8,128)(2,1)}), bf16[8,16,2048]{2,1,0:T(8,128)(2,1)S(1)}, u32[]{:S(2)}, u32[]{:S(2)}) %all-to-all-start.3) | async-done | bytes 524320 | tf_op jit(solution)/shard_map/all_to_all | solution.py:182
  192.4 2.3 %collective-permute-start.7 = (bf16[256,1152]{1,0:T(8,128)(2,1)}, bf16[256,1152]{1,0:T(8,128)(2,1)S(1)}, u32[]{:S(2)}, u32[]{:S(2)}) collective-permute-start(bf16[256,1152]{1,0:T(8,128)(2,1)} %get-tuple-element.29), channel_id=1, source_target_pairs={{0,128},{1,897},{2,130},{3,899},{4,132},{5,901},{6,134},{7,903},{8... | collective-permute-start | bytes 1769480 | tf_op jit(solution)/shard_map/ppermute | solution.py:38
  194.7 2.5 %collective-permute-start.6 = (bf16[256,1152]{1,0:T(8,128)(2,1)S(1)}, bf16[256,1152]{1,0:T(8,128)(2,1)S(1)}, u32[]{:S(2)}, u32[]{:S(2)}) collective-permute-start(bf16[256,1152]{1,0:T(8,128)(2,1)S(1)} %get-tuple-element.28), channel_id=1, source_target_pairs={{0,896},{1,129},{2,898},{3,131},{4,900},{5,133},{6,902},{7,135},{8... | collective-permute-start | bytes 1769480 | tf_op jit(solution)/shard_map/ppermute | solution.py:38
  198.0 9.3 %collective-permute-done.7 = bf16[256,1152]{1,0:T(8,128)(2,1)S(1)} collective-permute-done((bf16[256,1152]{1,0:T(8,128)(2,1)}, bf16[256,1152]{1,0:T(8,128)(2,1)S(1)}, u32[]{:S(2)}, u32[]{:S(2)}) %collective-permute-start.7) | collective-permute-done | bytes 589856 | tf_op jit(solution)/shard_map/ppermute | solution.py:38
  207.2 3.5 %collective-permute-done.6 = bf16[256,1152]{1,0:T(8,128)(2,1)S(1)} collective-permute-done((bf16[256,1152]{1,0:T(8,128)(2,1)S(1)}, bf16[256,1152]{1,0:T(8,128)(2,1)S(1)}, u32[]{:S(2)}, u32[]{:S(2)}) %collective-permute-start.6) | collective-permute-done | bytes 589856 | tf_op jit(solution)/shard_map/ppermute | solution.py:38
  210.8 1.3 fusion.1
  (26 shorter events, 9.4 us)
Async XLA Ops:
  0.6 0.8 copy-start.2
  1.5 0.8 copy-start.3
  2.3 0.7 copy-start.4
  3.0 0.7 copy-start.5
  3.7 0.7 copy-start.6
  31.8 1.3 copy-start.1
  33.1 76.7 %all-to-all-start.1 = ((bf16[16,16,4096]{2,1,0:T(8,128)(2,1)}), bf16[16,16,4096]{2,1,0:T(8,128)(2,1)S(1)}, u32[]{:S(2)}, u32[]{:S(2)}) async-start(bf16[16,16,4096]{2,1,0:T(8,128)(2,1)} %copy-done.1), calls=%async_computation.1 | async-start | bytes 4194304 | tf_op jit(solution)/shard_map/all_to_all | solution.py:182
  109.9 1.4 copy-start.7
  111.3 1.4 copy-start.8
  112.7 1.4 copy-start.9
  120.3 2.2 %copy-start = (bf16[8,256,1152]{2,1,0:T(8,128)(2,1)}, bf16[8,256,1152]{2,1,0:T(8,128)(2,1)S(1)}, u32[]{:S(2)}) copy-start(bf16[8,256,1152]{2,1,0:T(8,128)(2,1)S(1)} %shard_map.114) | copy-start | bytes 14155780
  122.6 13.5 %collective-permute-start.2 = (bf16[128,1152]{1,0:T(8,128)(2,1)S(1)}, bf16[128,1152]{1,0:T(8,128)(2,1)S(1)}, u32[]{:S(2)}, u32[]{:S(2)}) collective-permute-start(bf16[128,1152]{1,0:T(8,128)(2,1)S(1)} %get-tuple-element.40), channel_id=1, source_target_pairs={{0,896},{1,129},{2,898},{3,131},{4,900},{5,133},{6,902},{7,135},{8... | collective-permute-start | bytes 884744 | tf_op jit(solution)/shard_map/ppermute | solution.py:38
  125.9 10.4 %collective-permute-start = (bf16[128,1152]{1,0:T(8,128)(2,1)S(1)}, bf16[128,1152]{1,0:T(8,128)(2,1)S(1)}, u32[]{:S(2)}, u32[]{:S(2)}) collective-permute-start(bf16[128,1152]{1,0:T(8,128)(2,1)S(1)} %get-tuple-element.39), channel_id=1, source_target_pairs={{0,128},{1,897},{2,130},{3,899},{4,132},{5,901},{6,134},{7,903},{8... | collective-permute-start | bytes 884744 | tf_op jit(solution)/shard_map/ppermute | solution.py:38
  131.4 32.6 %all-to-all-start.2 = ((bf16[16,16,2048]{2,1,0:T(8,128)(2,1)}), bf16[16,16,2048]{2,1,0:T(8,128)(2,1)S(1)}, u32[]{:S(2)}, u32[]{:S(2)}) async-start(bf16[16,16,2048]{2,1,0:T(8,128)(2,1)} %bitcast.16), calls=%async_computation.2 | async-start | bytes 2097152 | tf_op jit(solution)/shard_map/all_to_all | solution.py:182
  137.6 14.0 %collective-permute-start.3 = (bf16[256,1152]{1,0:T(8,128)(2,1)S(1)}, bf16[256,1152]{1,0:T(8,128)(2,1)}, u32[]{:S(2)}, u32[]{:S(2)}) collective-permute-start(bf16[256,1152]{1,0:T(8,128)(2,1)S(1)} %pad_maximum_fusion.1), channel_id=1, source_target_pairs={{0,128},{1,897},{2,130},{3,899},{4,132},{5,901},{6,134},{7,903},{8... | collective-permute-start | bytes 1769480 | tf_op jit(solution)/shard_map/ppermute | solution.py:38
  143.3 13.4 %collective-permute-start.1 = (bf16[256,1152]{1,0:T(8,128)(2,1)}, bf16[256,1152]{1,0:T(8,128)(2,1)}, u32[]{:S(2)}, u32[]{:S(2)}) collective-permute-start(bf16[256,1152]{1,0:T(8,128)(2,1)} %pad_maximum_fusion), channel_id=1, source_target_pairs={{0,896},{1,129},{2,898},{3,131},{4,900},{5,133},{6,902},{7,135},{8... | collective-permute-start | bytes 1769480 | tf_op jit(solution)/shard_map/ppermute | solution.py:38
  164.1 14.0 %collective-permute-start.5 = (bf16[256,1152]{1,0:T(8,128)(2,1)S(1)}, bf16[256,1152]{1,0:T(8,128)(2,1)S(1)}, u32[]{:S(2)}, u32[]{:S(2)}) collective-permute-start(bf16[256,1152]{1,0:T(8,128)(2,1)S(1)} %get-tuple-element.24), channel_id=1, source_target_pairs={{0,896},{1,129},{2,898},{3,131},{4,900},{5,133},{6,902},{7,135},{8... | collective-permute-start | bytes 1769480 | tf_op jit(solution)/shard_map/ppermute | solution.py:38
  167.3 14.5 %collective-permute-start.4 = (bf16[256,1152]{1,0:T(8,128)(2,1)S(1)}, bf16[256,1152]{1,0:T(8,128)(2,1)}, u32[]{:S(2)}, u32[]{:S(2)}) collective-permute-start(bf16[256,1152]{1,0:T(8,128)(2,1)S(1)} %get-tuple-element.23), channel_id=1, source_target_pairs={{0,128},{1,897},{2,130},{3,899},{4,132},{5,901},{6,134},{7,903},{8... | collective-permute-start | bytes 1769480 | tf_op jit(solution)/shard_map/ppermute | solution.py:38
  170.9 21.4 %all-to-all-start.3 = ((bf16[8,16,2048]{2,1,0:T(8,128)(2,1)}), bf16[8,16,2048]{2,1,0:T(8,128)(2,1)S(1)}, u32[]{:S(2)}, u32[]{:S(2)}) async-start(bf16[8,16,2048]{2,1,0:T(8,128)(2,1)} %bitcast.19), calls=%async_computation.3 | async-start | bytes 1048576 | tf_op jit(solution)/shard_map/all_to_all | solution.py:182
  192.4 14.8 %collective-permute-start.7 = (bf16[256,1152]{1,0:T(8,128)(2,1)}, bf16[256,1152]{1,0:T(8,128)(2,1)S(1)}, u32[]{:S(2)}, u32[]{:S(2)}) collective-permute-start(bf16[256,1152]{1,0:T(8,128)(2,1)} %get-tuple-element.29), channel_id=1, source_target_pairs={{0,128},{1,897},{2,130},{3,899},{4,132},{5,901},{6,134},{7,903},{8... | collective-permute-start | bytes 1769480 | tf_op jit(solution)/shard_map/ppermute | solution.py:38
  194.7 16.0 %collective-permute-start.6 = (bf16[256,1152]{1,0:T(8,128)(2,1)S(1)}, bf16[256,1152]{1,0:T(8,128)(2,1)S(1)}, u32[]{:S(2)}, u32[]{:S(2)}) collective-permute-start(bf16[256,1152]{1,0:T(8,128)(2,1)S(1)} %get-tuple-element.28), channel_id=1, source_target_pairs={{0,896},{1,129},{2,898},{3,131},{4,900},{5,133},{6,902},{7,135},{8... | collective-permute-start | bytes 1769480 | tf_op jit(solution)/shard_map/ppermute | solution.py:38

commit v2 on v1

v2 whole, which is shorter than its diff:
```python
import functools

import jax
import jax.numpy as jnp
from jax import lax
from jax.experimental import pallas as pl
from jax.experimental.pallas import tpu as pltpu
from jax.sharding import PartitionSpec as P

F32 = jnp.float32
BF16 = jnp.bfloat16
LANES = 128


def contract(left, right, left_dim, right_dim):
    return lax.dot_general(
        left, right, (((left_dim,), (right_dim,)), ((), ())), preferred_element_type=F32
    )


def send_kernel(
    node_count, tokens_hbm, cot_hbm, ids_hbm, groups_hbm, gate_weight, sent, tokens, cotangent, expert_ids, node_groups, done
):
    loads = [
        pltpu.make_async_copy(ids_hbm, expert_ids, done.at[0]),
        pltpu.make_async_copy(groups_hbm, node_groups, done.at[1]),
        pltpu.make_async_copy(tokens_hbm, tokens, done.at[2]),
        pltpu.make_async_copy(cot_hbm, cotangent, done.at[3]),
    ]
    for load in loads:
        load.start()
    for load in loads:
        load.wait()
    group_count, tok_count, _ = sent.shape
    width = tokens.shape[1]
    choices, limit = expert_ids.shape[0], node_groups.shape[0]
    weights = gate_weight[...].astype(F32)
    expert = lax.broadcasted_iota(jnp.int32, (group_count * node_count, tok_count), 0)
    table = jnp.zeros(expert.shape, F32)
    for k in range(choices):
        table = table + jnp.where(expert_ids[k : k + 1, :] == expert, weights[k : k + 1, :], 0.0)
    for g in range(group_count):
        picked = node_groups[0:1, :] == g
        for j in range(1, limit):
            picked = picked | (node_groups[j : j + 1, :] == g)
        block = jnp.where(picked, table[g * node_count : (g + 1) * node_count, :], 0.0)
        sent[g, :, :width] = tokens[...]
        sent[g, :, width : 2 * width] = cotangent[...]
        sent[g, :, 2 * width :] = jnp.zeros((tok_count, LANES), BF16)
        sent[g, :node_count, 2 * width : 2 * width + tok_count] = block.astype(BF16)


def slot_kernel(arrived, slots_hbm, select, slots, done):
    group_count, tok_count, _ = arrived.shape
    node_count, capacity, width = slots.shape
    width = width // 2
    family = group_count * tok_count
    table = [arrived[g, :node_count, 2 * width : 2 * width + tok_count] for g in range(group_count)]
    table = jnp.concatenate([part.astype(F32) for part in table], axis=1)
    routed = table > 0
    row = lax.broadcasted_iota(jnp.int32, (family, family), 0)
    column = lax.broadcasted_iota(jnp.int32, (family, family), 1)
    earlier = jnp.where(row < column, 1.0, 0.0).astype(BF16)
    position = contract(jnp.where(routed, 1.0, 0.0).astype(BF16), earlier, 1, 0)
    place = jnp.where(routed, position, -1.0)[:, None, :]
    slot = lax.broadcasted_iota(jnp.int32, (node_count, capacity, family), 1).astype(F32)
    taken = place == slot
    picks = jnp.where(taken, 1.0, 0.0).reshape(node_count * capacity, family).astype(BF16)
    weighted = jnp.where(taken, table[:, None, :], 0.0).reshape(node_count * capacity, family).astype(BF16)
    select[...] = picks
    cut = width // 2
    stores = []
    for start in range(0, 2 * width, cut):
        part = slice(start, start + cut)
        block = arrived[:, :, part].reshape(family, cut)
        out = contract(picks if start < width else weighted, block, 1, 0)
        slots[:, :, part] = out.reshape(node_count, capacity, cut).astype(BF16)
        stores.append(pltpu.make_async_copy(slots.at[:, :, part], slots_hbm.at[:, :, part], done.at[len(stores)]))
        stores[-1].start()
    for store in stores:
        store.wait()


def expert_kernel(
    landed, gate_hbm, up_hbm, down_hbm, partial_hbm, pair_grad, gate_proj, up_proj, down_proj, partial, done, stored
):
    width, hid = gate_proj.shape
    count, cut, _ = partial.shape
    loads = [
        pltpu.make_async_copy(gate_hbm, gate_proj, done.at[0]),
        pltpu.make_async_copy(up_hbm, up_proj, done.at[1]),
        pltpu.make_async_copy(down_hbm, down_proj, done.at[2]),
    ]
    for load in loads:
        load.start()
    loads[0].wait()
    gate_value = contract(landed[:, :width], gate_proj[...], 1, 0)
    loads[1].wait()
    up_value = contract(landed[:, :width], up_proj[...], 1, 0)
    sigmoid = 1.0 / (1.0 + jnp.exp(-gate_value))
    silu = gate_value * sigmoid
    hidden = (silu * up_value).astype(BF16)
    loads[2].wait()
    hidden_grad = contract(landed[:, width:], down_proj[...], 1, 1)
    slope = up_value * sigmoid * (1.0 + gate_value * (1.0 - sigmoid))
    pair_grad[:, :hid] = (hidden_grad * slope).astype(BF16)
    pair_grad[:, hid:] = (hidden_grad * silu).astype(BF16)
    stores = []
    for block in range(count):
        rows = landed[:, block * cut : (block + 1) * cut]
        cot_rows = landed[:, width + block * cut : width + (block + 1) * cut]
        partial[block, :, : 2 * hid] = contract(rows, pair_grad[...], 0, 0).astype(BF16)
        partial[block, :, 2 * hid :] = contract(cot_rows, hidden, 0, 0).astype(BF16)
        stores.append(pltpu.make_async_copy(partial.at[block], partial_hbm.at[block], stored.at[block]))
        stores[-1].start()
    for store in stores:
        store.wait()


def route_kernel(pair_grad, gate_proj, up_proj, route_grad):
    width, hid = gate_proj.shape
    cut = width // 4
    for start in range(0, width, cut):
        part = slice(start, start + cut)
        grad = contract(pair_grad[:, :hid], gate_proj[part, :], 1, 1)
        grad = grad + contract(pair_grad[:, hid:], up_proj[part, :], 1, 1)
        route_grad[:, part] = grad.astype(BF16)


def run(kernel, out, *args, flops=0, **kwargs):
    held = sum(x.size * x.dtype.itemsize for x in (*args, *out))
    return pl.pallas_call(
        kernel,
        out_shape=out,
        cost_estimate=pl.CostEstimate(flops=flops, bytes_accessed=held, transcendentals=0),
        compiler_params=pltpu.CompilerParams(vmem_limit_bytes=40 * 1024 * 1024),
        **kwargs,
    )(*args)


def shards(tokens, cotangent, expert_ids, node_groups, gate_weight, gate_proj, up_proj, down_proj):
    data_count = lax.axis_size("dp")
    group_count = lax.axis_size("group")
    node_count = lax.axis_size("node")
    tok_count, width = tokens.shape
    hid = down_proj.shape[1]
    per_group = expert_ids.shape[1] // node_groups.shape[1]
    family = group_count * tok_count
    capacity = (per_group * family + node_count - 1) // node_count
    count = node_count * capacity
    dot_flops = 2 * count * width * hid

    def shape(*dims):
        return jax.ShapeDtypeStruct(dims, BF16)

    def over(axis, blocks):
        return lax.all_to_all(blocks, axis, split_axis=0, concat_axis=0, tiled=True)

    here = pl.BlockSpec(memory_space=pltpu.VMEM)
    far = pl.BlockSpec(memory_space=pltpu.HBM)
    (sent,) = run(
        functools.partial(send_kernel, node_count),
        (shape(group_count, tok_count, 2 * width + LANES),),
        tokens, cotangent, expert_ids.T, node_groups.T, gate_weight.T,
        in_specs=[far, far, far, far, here],
        out_specs=[here],
        scratch_shapes=[
            pltpu.VMEM((tok_count, width), BF16),
            pltpu.VMEM((tok_count, width), BF16),
            pltpu.VMEM(expert_ids.shape[::-1], jnp.int32),
            pltpu.VMEM(node_groups.shape[::-1], jnp.int32),
            pltpu.SemaphoreType.DMA((4,)),
        ],
    )
    arrived = over("group", sent)
    slots, select = run(
        slot_kernel,
        (shape(node_count, capacity, 2 * width), shape(count, family)),
        arrived,
        flops=4 * count * family * width,
        in_specs=[here],
        out_specs=[far, here],
        scratch_shapes=[pltpu.VMEM((node_count, capacity, 2 * width), BF16), pltpu.SemaphoreType.DMA((4,))],
    )
    landed = over("node", slots).reshape(count, 2 * width)
    partial, pair_grad = run(
        expert_kernel,
        (shape(data_count, width // data_count, 3 * hid), shape(count, 2 * hid)),
        landed, gate_proj[0], up_proj[0], down_proj[0],
        flops=6 * dot_flops,
        in_specs=[here, far, far, far],
        out_specs=[far, here],
        scratch_shapes=[
            pltpu.VMEM((width, hid), BF16),
            pltpu.VMEM((width, hid), BF16),
            pltpu.VMEM((hid, width), BF16),
            pltpu.VMEM((data_count, width // data_count, 3 * hid), BF16),
            pltpu.SemaphoreType.DMA((3,)),
            pltpu.SemaphoreType.DMA((data_count,)),
        ],
    )
    total = lax.psum_scatter(partial.reshape(width, 3 * hid), "dp", scatter_dimension=0, tiled=True)

    (route_grad,) = run(
        route_kernel, (shape(count, width),), pair_grad, gate_proj[0], up_proj[0], flops=2 * dot_flops
    )
    returned = over("node", route_grad.reshape(node_count, capacity, width))
    group_grad = contract(select, returned.reshape(count, width), 0, 0).astype(BF16)
    home = over("group", group_grad.reshape(group_count, tok_count, width))
    grad_tokens = jnp.sum(home.astype(F32), axis=0).astype(BF16)
    return (
        grad_tokens,
        total[None, :, :hid],
        total[None, :, hid : 2 * hid],
        total[:, 2 * hid :].T[None],
    )


def solution(mesh):
    rows = P(("dp", "group", "node"), None)
    experts = P(("group", "node"), None, None)
    return jax.shard_map(
        shards,
        mesh=mesh,
        in_specs=(rows,) * 5 + (experts,) * 3,
        out_specs=(
            rows,
            P(("group", "node"), "dp", None),
            P(("group", "node"), "dp", None),
            P(("group", "node"), None, "dp"),
        ),
        check_vma=False,
    )
```

time: 215 us -> 195 us (0.907)
  blocking collectives: 26.4 us -> 156 us
  waiting for transfers between devices: 94.3 us -> 4.37 us
  starting transfers between devices: 62.1 us -> 0.04 us
  between operations: 0.88 us -> 14.1 us
  other arithmetic: 8.46 us -> 0.7 us
  local copies, waits for them, and re-layouts: 13.2 us -> 8.62 us
  Pallas kernels: 7.25 us -> 9.85 us
    all_to_all x1 -> x4, blocking collectives: 26.4 us -> 156 us  [over(): return lax.all_to_all(blocks, axis, split_axis=0, concat_axis=0, tiled=True)]
    all_to_all x3 -> x0, waiting for transfers between devices: 62.5 us -> none  [over(): return lax.all_to_all(blocks, axis, split_axis=0, concat_axis=0, tiled=True)]
    all_to_all x3 -> x0, starting transfers between devices: 36 us -> none  [over(): return lax.all_to_all(blocks, axis, split_axis=0, concat_axis=0, tiled=True)]
    ppermute x8 -> x0, waiting for transfers between devices: 31.8 us -> none  [exchange(): return lax.ppermute(block, ('dp', 'node'), pairs)]
    ppermute x8 -> x0, starting transfers between devices: 26.1 us -> none  [exchange(): return lax.ppermute(block, ('dp', 'node'), pairs)]
    convert_element_type x4 -> x0, other arithmetic: 6.86 us -> none  [the longest x3 5.58 us: add(): return (left.astype(F32) + right.astype(F32)).astype(BF16)]
    unnamed x21 -> x23, local copies, waits for them, and re-layouts: 12.2 us -> 6.7 us
    reduce_scatter x0 -> x1, waiting for transfers between devices: none -> 4.35 us  [shards(): lax.psum_scatter(partial.reshape(width, 3 * hid), 'dp', scatter_dimension...]
  transfers between devices with their start and end apart: 11 -> 1, of which waited for: 10 -> 1; matrix products, arithmetic and copies ran while one was open for 4% -> 1% of each run, Pallas kernels for 0% -> 1%
where the time goes in v2:
time: 195 us; the launch traced here: 194 us
  blocking collectives  156 us (80%)
  between operations  14.1 us (7%)
  Pallas kernels  9.85 us (5%)
  local copies, waits for them, and re-layouts  8.62 us (4%)
  waiting for transfers between devices  4.37 us (2%)
    all_to_all x4, blocking collectives, over(): return lax.all_to_all(blocks, axis, split_axis=0, concat_axis=0, tiled=True)  156 us
    pallas_call x4, Pallas kernels, run(): pl.pallas_call(kernel, out_shape=out, cost_estimate=pl.CostEstimate(flops...  9.85 us
    unnamed x23, local copies, waits for them, and re-layouts  6.7 us
    reduce_scatter x1, waiting for transfers between devices, shards(): lax.psum_scatter(partial.reshape(width, 3 * hid), 'dp', scatter_dimension...  4.35 us
  transfers between devices with their start and end apart: 1, of which 1 were waited for; matrix products, arithmetic and copies ran while one was open for 1% of the time, Pallas kernels for 1%

profile of v2, /device:TPU:1, one launch (start us, length us, event | category | flops | bytes accessed | tf_op | source)
XLA Modules:
  0.0 194.1 jit_solution(11120575931921040839)
XLA Ops:
  7.2 0.0 reduce-scatter.2.cloned.1.call-start
  7.2 0.0 copy-start.3
  7.2 0.8 copy-done.3
  8.1 0.8 copy-done.4
  8.9 0.7 copy-done.7
  9.6 0.7 copy-done.8
  10.3 0.7 copy-done.9
  10.9 0.3 shard_map.111
  11.3 26.3 %all_to_all.20.arrived = bf16[8,16,4224]{2,1,0:T(8,128)(2,1)S(1)} all-to-all(bf16[8,16,4224]{2,1,0:T(8,128)(2,1)S(1)} %shard_map.111), channel_id=1, replica_groups=mesh['dp'=8,'group'=8,'node'=16] {'group'}, dimensions={0} | all-to-all | bytes 2162688 | tf_op jit(solution)/shard_map/all_to_all | solution.py:157
  37.6 1.6 shard_map.112
  39.2 0.0 copy-start.5
  39.2 0.0 copy-start.1
  39.2 0.0 copy-start.2
  39.2 78.9 %all_to_all.21 = bf16[16,16,4096]{2,1,0:T(8,128)(2,1)S(1)} all-to-all(bf16[16,16,4096]{2,1,0:T(8,128)(2,1)S(1)} %get-tuple-element.9), channel_id=1, replica_groups=mesh['dp'=8,'group'=8,'node'=16] {'node'}, dimensions={0} | all-to-all | bytes 4194304 | tf_op jit(solution)/shard_map/all_to_all | solution.py:157
  118.2 0.0 copy-done.5
  118.2 0.0 copy-done.10
  118.2 0.0 copy-done.1
  118.2 0.0 copy-done.2
  118.2 6.7 %shard_map.113 = (bf16[8,256,1152]{2,1,0:T(8,128)(2,1)S(1)}, bf16[256,768]{1,0:T(8,128)(2,1)S(1)}) custom-call(bf16[256,4096]{1,0:T(8,128)(2,1)S(1)} %bitcast.23, bf16[2048,384]{1,0:T(8,128)(2,1)S(1)} %bitcast.24, bf16[2048,384]{1,0:T(8,128)(2,1)S(1)} %bitcast.26, bf16[384,2048]{1,0:T(8,128)(2,1)S(1)} %bitcast.31), custom_call_target="tpu_custom_call" | custom-call | flops 2415919104 | bytes 11927552 | tf_op jit(solution)/shard_map/pallas_call | solution.py:132
  124.9 0.0 copy-start
  124.9 2.1 %copy-done = bf16[8,256,1152]{2,1,0:T(8,128)(2,1)} copy-done((bf16[8,256,1152]{2,1,0:T(8,128)(2,1)}, bf16[8,256,1152]{2,1,0:T(8,128)(2,1)S(1)}, u32[]{:S(2)}) %copy-start) | copy-done | bytes 4718616
  127.0 0.0 reduce-scatter.2.cloned.1.call-update
  127.0 1.3 shard_map.114
  128.3 0.0 copy-start.6
  128.3 31.4 %all_to_all.22 = bf16[16,16,2048]{2,1,0:T(8,128)(2,1)S(1)} all-to-all(bf16[16,16,2048]{2,1,0:T(8,128)(2,1)S(1)} %bitcast.22), channel_id=1, replica_groups=mesh['dp'=8,'group'=8,'node'=16] {'node'}, dimensions={0} | all-to-all | bytes 2097152 | tf_op jit(solution)/shard_map/all_to_all | solution.py:157
  159.7 0.0 copy-done.6
  159.7 0.3 convolution_convert_fusion
  160.1 19.4 %all_to_all.23 = bf16[8,16,2048]{2,1,0:T(8,128)(2,1)S(1)} all-to-all(bf16[8,16,2048]{2,1,0:T(8,128)(2,1)S(1)} %bitcast.33), channel_id=1, replica_groups=mesh['dp'=8,'group'=8,'node'=16] {'group'}, dimensions={0} | all-to-all | bytes 1048576 | tf_op jit(solution)/shard_map/all_to_all | solution.py:157
  179.5 0.7 reduce_sum.12
  180.2 4.4 %reduce-scatter.2.cloned.1.call-done = bf16[256,1152]{1,0:T(8,128)(2,1)} async-done(((bf16[2048,1152]{1,0:T(8,128)(2,1)}), bf16[256,1152]{1,0:T(8,128)(2,1)}) %reduce-scatter.2.cloned.1.call-update) | async-done | bytes 589840 | tf_op jit(solution)/shard_map/reduce_scatter | solution.py:202
  184.5 1.9 slice_bitcast_fusion
  186.5 0.8 copy.13
  (5 shorter events, 0.0 us)
Async XLA Ops:
  7.2 177.4 %reduce-scatter.2.cloned.1.call-start = ((), (), s32[]{:S(2)}) async-start(), calls=%async_computation.5 | async-start | bytes 5308416 | tf_op jit(solution)/shard_map/reduce_scatter | solution.py:202
  7.2 0.8 copy-start.3
  8.1 0.8 copy-start.4
  8.9 0.7 copy-start.7
  9.6 0.7 copy-start.8
  10.3 0.7 copy-start.9
  37.6 80.6 %copy-start.10 = (bf16[1,384,2048]{2,1,0:T(8,128)(2,1)S(1)}, bf16[1,384,2048]{2,1,0:T(8,128)(2,1)}, u32[]{:S(2)}) copy-start(bf16[1,384,2048]{2,1,0:T(8,128)(2,1)} %param.15) | copy-start | bytes 4718596
  39.2 79.0 %copy-start.5 = (bf16[256,128]{1,0:T(8,128)(2,1)}, bf16[256,128]{1,0:T(8,128)(2,1)S(1)}, u32[]{:S(2)}) copy-start(bf16[256,128]{1,0:T(8,128)(2,1)S(1)} %get-tuple-element.8) | copy-start | bytes 196612
  39.2 79.0 %copy-start.1 = (bf16[1,2048,384]{2,1,0:T(8,128)(2,1)S(1)}, bf16[1,2048,384]{2,1,0:T(8,128)(2,1)}, u32[]{:S(2)}) copy-start(bf16[1,2048,384]{2,1,0:T(8,128)(2,1)} %param.13) | copy-start | bytes 4718596
  39.2 78.9 %copy-start.2 = (bf16[1,2048,384]{2,1,0:T(8,128)(2,1)S(1)}, bf16[1,2048,384]{2,1,0:T(8,128)(2,1)}, u32[]{:S(2)}) copy-start(bf16[1,2048,384]{2,1,0:T(8,128)(2,1)} %param.14) | copy-start | bytes 4718596
  124.9 2.1 %copy-start = (bf16[8,256,1152]{2,1,0:T(8,128)(2,1)}, bf16[8,256,1152]{2,1,0:T(8,128)(2,1)S(1)}, u32[]{:S(2)}) copy-start(bf16[8,256,1152]{2,1,0:T(8,128)(2,1)S(1)} %get-tuple-element.11) | copy-start | bytes 14155780
  128.3 31.4 %copy-start.6 = (bf16[256,128]{1,0:T(8,128)(2,1)S(1)}, bf16[256,128]{1,0:T(8,128)(2,1)}, u32[]{:S(2)}) copy-start(bf16[256,128]{1,0:T(8,128)(2,1)} %copy-done.5) | copy-start | bytes 196612
Sparse Core Ops, SparseCore 0:
  127.2 57.3 reduce-scatter.1

commit v3 on v2

--- a/solution.py
+++ b/solution.py
@@ -10,6 +10,8 @@
 F32 = jnp.float32
 BF16 = jnp.bfloat16
 LANES = 128
+MIB = 1024 * 1024
+ALONE = 63 * MIB
 
 
 def contract(left, right, left_dim, right_dim):
@@ -18,19 +20,7 @@
     )
 
 
-def send_kernel(
-    node_count, tokens_hbm, cot_hbm, ids_hbm, groups_hbm, gate_weight, sent, tokens, cotangent, expert_ids, node_groups, done
-):
-    loads = [
-        pltpu.make_async_copy(ids_hbm, expert_ids, done.at[0]),
-        pltpu.make_async_copy(groups_hbm, node_groups, done.at[1]),
-        pltpu.make_async_copy(tokens_hbm, tokens, done.at[2]),
-        pltpu.make_async_copy(cot_hbm, cotangent, done.at[3]),
-    ]
-    for load in loads:
-        load.start()
-    for load in loads:
-        load.wait()
+def send_kernel(node_count, tokens, cotangent, expert_ids, node_groups, gate_weight, sent):
     group_count, tok_count, _ = sent.shape
     width = tokens.shape[1]
     choices, limit = expert_ids.shape[0], node_groups.shape[0]
@@ -50,7 +40,7 @@
         sent[g, :node_count, 2 * width : 2 * width + tok_count] = block.astype(BF16)
 
 
-def slot_kernel(arrived, slots_hbm, select, slots, done):
+def slot_kernel(arrived, slots, select):
     group_count, tok_count, _ = arrived.shape
     node_count, capacity, width = slots.shape
     width = width // 2
@@ -69,38 +59,39 @@
     weighted = jnp.where(taken, table[:, None, :], 0.0).reshape(node_count * capacity, family).astype(BF16)
     select[...] = picks
     cut = width // 2
-    stores = []
     for start in range(0, 2 * width, cut):
         part = slice(start, start + cut)
         block = arrived[:, :, part].reshape(family, cut)
         out = contract(picks if start < width else weighted, block, 1, 0)
         slots[:, :, part] = out.reshape(node_count, capacity, cut).astype(BF16)
-        stores.append(pltpu.make_async_copy(slots.at[:, :, part], slots_hbm.at[:, :, part], done.at[len(stores)]))
-        stores[-1].start()
-    for store in stores:
-        store.wait()
 
 
 def expert_kernel(
-    landed, gate_hbm, up_hbm, down_hbm, partial_hbm, pair_grad, gate_proj, up_proj, down_proj, partial, done, stored
+    landed_hbm, gate_hbm, up_hbm, down_hbm, partial_hbm, pair_grad,
+    landed, gate_proj, up_proj, down_proj, partial, done, stored,
 ):
     width, hid = gate_proj.shape
     count, cut, _ = partial.shape
+    left, right = (slice(None), slice(0, width)), (slice(None), slice(width, 2 * width))
     loads = [
-        pltpu.make_async_copy(gate_hbm, gate_proj, done.at[0]),
-        pltpu.make_async_copy(up_hbm, up_proj, done.at[1]),
-        pltpu.make_async_copy(down_hbm, down_proj, done.at[2]),
+        pltpu.make_async_copy(landed_hbm.at[left], landed.at[left], done.at[0]),
+        pltpu.make_async_copy(gate_hbm, gate_proj, done.at[1]),
+        pltpu.make_async_copy(up_hbm, up_proj, done.at[2]),
+        pltpu.make_async_copy(landed_hbm.at[right], landed.at[right], done.at[3]),
+        pltpu.make_async_copy(down_hbm, down_proj, done.at[4]),
     ]
     for load in loads:
         load.start()
     loads[0].wait()
+    loads[1].wait()
     gate_value = contract(landed[:, :width], gate_proj[...], 1, 0)
-    loads[1].wait()
+    loads[2].wait()
     up_value = contract(landed[:, :width], up_proj[...], 1, 0)
     sigmoid = 1.0 / (1.0 + jnp.exp(-gate_value))
     silu = gate_value * sigmoid
     hidden = (silu * up_value).astype(BF16)
-    loads[2].wait()
+    loads[3].wait()
+    loads[4].wait()
     hidden_grad = contract(landed[:, width:], down_proj[...], 1, 1)
     slope = up_value * sigmoid * (1.0 + gate_value * (1.0 - sigmoid))
     pair_grad[:, :hid] = (hidden_grad * slope).astype(BF16)
@@ -127,13 +118,20 @@
         route_grad[:, part] = grad.astype(BF16)
 
 
-def run(kernel, out, *args, flops=0, **kwargs):
+def split_kernel(total, gate_out, up_out, down_out):
+    hid = gate_out.shape[2]
+    gate_out[0] = total[:, :hid]
+    up_out[0] = total[:, hid : 2 * hid]
+    down_out[0] = total[:, 2 * hid :].T
+
+
+def run(kernel, out, *args, flops=0, vmem=40 * MIB, **kwargs):
     held = sum(x.size * x.dtype.itemsize for x in (*args, *out))
     return pl.pallas_call(
         kernel,
         out_shape=out,
         cost_estimate=pl.CostEstimate(flops=flops, bytes_accessed=held, transcendentals=0),
-        compiler_params=pltpu.CompilerParams(vmem_limit_bytes=40 * 1024 * 1024),
+        compiler_params=pltpu.CompilerParams(vmem_limit_bytes=vmem),
         **kwargs,
     )(*args)
 
@@ -162,15 +160,7 @@
         functools.partial(send_kernel, node_count),
         (shape(group_count, tok_count, 2 * width + LANES),),
         tokens, cotangent, expert_ids.T, node_groups.T, gate_weight.T,
-        in_specs=[far, far, far, far, here],
-        out_specs=[here],
-        scratch_shapes=[
-            pltpu.VMEM((tok_count, width), BF16),
-            pltpu.VMEM((tok_count, width), BF16),
-            pltpu.VMEM(expert_ids.shape[::-1], jnp.int32),
-            pltpu.VMEM(node_groups.shape[::-1], jnp.int32),
-            pltpu.SemaphoreType.DMA((4,)),
-        ],
+        vmem=ALONE,
     )
     arrived = over("group", sent)
     slots, select = run(
@@ -178,9 +168,6 @@
         (shape(node_count, capacity, 2 * width), shape(count, family)),
         arrived,
         flops=4 * count * family * width,
-        in_specs=[here],
-        out_specs=[far, here],
-        scratch_shapes=[pltpu.VMEM((node_count, capacity, 2 * width), BF16), pltpu.SemaphoreType.DMA((4,))],
     )
     landed = over("node", slots).reshape(count, 2 * width)
     partial, pair_grad = run(
@@ -188,14 +175,16 @@
         (shape(data_count, width // data_count, 3 * hid), shape(count, 2 * hid)),
         landed, gate_proj[0], up_proj[0], down_proj[0],
         flops=6 * dot_flops,
-        in_specs=[here, far, far, far],
+        vmem=ALONE,
+        in_specs=[far] * 4,
         out_specs=[far, here],
         scratch_shapes=[
+            pltpu.VMEM((count, 2 * width), BF16),
             pltpu.VMEM((width, hid), BF16),
             pltpu.VMEM((width, hid), BF16),
             pltpu.VMEM((hid, width), BF16),
             pltpu.VMEM((data_count, width // data_count, 3 * hid), BF16),
-            pltpu.SemaphoreType.DMA((3,)),
+            pltpu.SemaphoreType.DMA((5,)),
             pltpu.SemaphoreType.DMA((data_count,)),
         ],
     )
@@ -208,12 +197,11 @@
     group_grad = contract(select, returned.reshape(count, width), 0, 0).astype(BF16)
     home = over("group", group_grad.reshape(group_count, tok_count, width))
     grad_tokens = jnp.sum(home.astype(F32), axis=0).astype(BF16)
-    return (
-        grad_tokens,
-        total[None, :, :hid],
-        total[None, :, hid : 2 * hid],
-        total[:, 2 * hid :].T[None],
-    )
+    cut = width // data_count
+    gate_out, up_out, down_out = run(
+        split_kernel, (shape(1, cut, hid), shape(1, cut, hid), shape(1, hid, cut)), total, vmem=ALONE
+    )
+    return grad_tokens, gate_out, up_out, down_out
 
 
 def solution(mesh):

time: 195 us -> 189 us (0.969)
  local copies, waits for them, and re-layouts: 8.62 us -> 1.91 us
  Pallas kernels: 9.85 us -> 13.3 us
    unnamed x23 -> x10, local copies, waits for them, and re-layouts: 6.7 us -> 1.91 us
    pallas_call x4 -> x5, Pallas kernels: 9.85 us -> 13.3 us  [run(): pl.pallas_call(kernel, out_shape=out, cost_estimate=pl.CostEstimate(flops...]
where the time goes in v3:
time: 189 us
  blocking collectives  156 us (83%)
  between operations  14.1 us (7%)
  Pallas kernels  13.3 us (7%)
  waiting for transfers between devices  2.45 us (1%)
  local copies, waits for them, and re-layouts  1.91 us (1%)
    all_to_all x4, blocking collectives, over(): return lax.all_to_all(blocks, axis, split_axis=0, concat_axis=0, tiled=True)  156 us
    pallas_call x5, Pallas kernels, run(): pl.pallas_call(kernel, out_shape=out, cost_estimate=pl.CostEstimate(flops...  13.3 us
  transfers between devices with their start and end apart: 1, of which 1 were waited for; matrix products, arithmetic and copies ran while one was open for 1% of the time, Pallas kernels for 1%

profile of v3, /device:TPU:1, one launch (start us, length us, event | category | flops | bytes accessed | tf_op | source)
XLA Modules:
  0.0 189.0 jit_solution(537812552605130187)
XLA Ops:
  7.2 0.0 reduce-scatter.2.cloned.1.call-start
  7.2 2.0 %shard_map.111 = bf16[8,16,4224]{2,1,0:T(8,128)(2,1)} custom-call(bf16[16,2048]{1,0:T(8,128)(2,1)} %tokens.1, bf16[16,2048]{1,0:T(8,128)(2,1)} %cotangent.1, s32[8,16]{1,0:T(8,128)} %bitcast.22, s32[4,16]{1,0:T(4,128)} %bitcast.23, bf16[8,16]{1,0:T(8,128)(2,1)} %bitcast.24), custom_call_target="tpu_custom_call" | custom-call | bytes 1213440 | tf_op jit(solution)/shard_map/pallas_call | solution.py:130
  9.2 25.3 %all_to_all.20.arrived = bf16[8,16,4224]{2,1,0:T(8,128)(2,1)S(1)} all-to-all(bf16[8,16,4224]{2,1,0:T(8,128)(2,1)} %shard_map.111), channel_id=1, replica_groups=mesh['dp'=8,'group'=8,'node'=16] {'group'}, dimensions={0} | all-to-all | bytes 2162688 | tf_op jit(solution)/shard_map/all_to_all | solution.py:155
  34.5 0.9 shard_map.112
  35.4 0.0 copy-start.3
  35.4 80.0 %all_to_all.21 = bf16[16,16,4096]{2,1,0:T(8,128)(2,1)} all-to-all(bf16[16,16,4096]{2,1,0:T(8,128)(2,1)S(1)} %get-tuple-element.12), channel_id=1, replica_groups=mesh['dp'=8,'group'=8,'node'=16] {'node'}, dimensions={0} | all-to-all | bytes 4194304 | tf_op jit(solution)/shard_map/all_to_all | solution.py:155
  115.4 0.0 copy-done.3
  115.4 7.3 %shard_map.113 = (bf16[8,256,1152]{2,1,0:T(8,128)(2,1)}, bf16[256,768]{1,0:T(8,128)(2,1)}) custom-call(bf16[256,4096]{1,0:T(8,128)(2,1)} %bitcast.21, bf16[2048,384]{1,0:T(8,128)(2,1)} %bitcast.14, bf16[2048,384]{1,0:T(8,128)(2,1)} %bitcast.16, bf16[384,2048]{1,0:T(8,128)(2,1)} %bitcast.25), custom_call_target="tpu_custom_call" | custom-call | flops 2415919104 | bytes 11927552 | tf_op jit(solution)/shard_map/pallas_call | solution.py:130
  122.7 0.0 copy-start
  122.7 0.0 copy-start.1
  122.7 0.0 copy-start.2
  122.7 0.0 reduce-scatter.2.cloned.1.call-update
  122.7 1.4 copy-done
  124.1 0.5 copy-done.1
  124.6 0.1 copy-done.2
  124.6 1.3 shard_map.114
  125.9 0.0 copy-start.4
  125.9 31.4 %all_to_all.22 = bf16[16,16,2048]{2,1,0:T(8,128)(2,1)S(1)} all-to-all(bf16[16,16,2048]{2,1,0:T(8,128)(2,1)S(1)} %bitcast.13), channel_id=1, replica_groups=mesh['dp'=8,'group'=8,'node'=16] {'node'}, dimensions={0} | all-to-all | bytes 2097152 | tf_op jit(solution)/shard_map/all_to_all | solution.py:155
  157.3 0.0 copy-done.4
  157.3 0.3 convolution_convert_fusion
  157.7 19.4 %all_to_all.23 = bf16[8,16,2048]{2,1,0:T(8,128)(2,1)S(1)} all-to-all(bf16[8,16,2048]{2,1,0:T(8,128)(2,1)S(1)} %bitcast.20), channel_id=1, replica_groups=mesh['dp'=8,'group'=8,'node'=16] {'group'}, dimensions={0} | all-to-all | bytes 1048576 | tf_op jit(solution)/shard_map/all_to_all | solution.py:155
  177.1 0.7 reduce_sum.12
  177.8 2.4 %reduce-scatter.2.cloned.1.call-done.total = bf16[256,1152]{1,0:T(8,128)(2,1)} async-done(((bf16[2048,1152]{1,0:T(8,128)(2,1)}), bf16[256,1152]{1,0:T(8,128)(2,1)}) %reduce-scatter.2.cloned.1.call-update) | async-done | bytes 589840 | tf_op jit(solution)/shard_map/reduce_scatter | solution.py:191
  180.2 1.9 %shard_map.115 = (bf16[1,256,384]{2,1,0:T(8,128)(2,1)}, bf16[1,256,384]{2,1,0:T(8,128)(2,1)}, bf16[1,384,256]{2,1,0:T(8,128)(2,1)}) custom-call(bf16[256,1152]{1,0:T(8,128)(2,1)} %reduce-scatter.2.cloned.1.call-done.total), custom_call_target="tpu_custom_call" | custom-call | bytes 1179648 | tf_op jit(solution)/shard_map/pallas_call | solution.py:130
Async XLA Ops:
  7.2 173.1 %reduce-scatter.2.cloned.1.call-start = ((), (), s32[]{:S(2)}) async-start(), calls=%async_computation.5 | async-start | bytes 5308416 | tf_op jit(solution)/shard_map/reduce_scatter | solution.py:191
  35.4 80.0 %copy-start.3 = (bf16[256,128]{1,0:T(8,128)(2,1)}, bf16[256,128]{1,0:T(8,128)(2,1)S(1)}, u32[]{:S(2)}) copy-start(bf16[256,128]{1,0:T(8,128)(2,1)S(1)} %get-tuple-element.11) | copy-start | bytes 196612
  122.7 1.4 copy-start
  122.7 1.9 copy-start.1
  122.7 1.9 %copy-start.2 = (bf16[256,768]{1,0:T(8,128)(2,1)S(1)}, bf16[256,768]{1,0:T(8,128)(2,1)}, u32[]{:S(2)}) copy-start(bf16[256,768]{1,0:T(8,128)(2,1)} %get-tuple-element.13.pair_grad) | copy-start | bytes 1179652
  125.9 31.4 %copy-start.4 = (bf16[256,128]{1,0:T(8,128)(2,1)S(1)}, bf16[256,128]{1,0:T(8,128)(2,1)}, u32[]{:S(2)}) copy-start(bf16[256,128]{1,0:T(8,128)(2,1)} %copy-done.3) | copy-start | bytes 196612
Sparse Core Ops, SparseCore 0:
  122.9 57.3 reduce-scatter.1

commit v4 on v3

--- a/solution.py
+++ b/solution.py
@@ -12,6 +12,7 @@
 LANES = 128
 MIB = 1024 * 1024
 ALONE = 63 * MIB
+BESIDE = 44 * MIB
 
 
 def contract(left, right, left_dim, right_dim):
@@ -67,31 +68,15 @@
 
 
 def expert_kernel(
-    landed_hbm, gate_hbm, up_hbm, down_hbm, partial_hbm, pair_grad,
-    landed, gate_proj, up_proj, down_proj, partial, done, stored,
+    landed, gate_proj, up_proj, down_proj, partial_hbm, pair_grad, partial, stored
 ):
     width, hid = gate_proj.shape
     count, cut, _ = partial.shape
-    left, right = (slice(None), slice(0, width)), (slice(None), slice(width, 2 * width))
-    loads = [
-        pltpu.make_async_copy(landed_hbm.at[left], landed.at[left], done.at[0]),
-        pltpu.make_async_copy(gate_hbm, gate_proj, done.at[1]),
-        pltpu.make_async_copy(up_hbm, up_proj, done.at[2]),
-        pltpu.make_async_copy(landed_hbm.at[right], landed.at[right], done.at[3]),
-        pltpu.make_async_copy(down_hbm, down_proj, done.at[4]),
-    ]
-    for load in loads:
-        load.start()
-    loads[0].wait()
-    loads[1].wait()
     gate_value = contract(landed[:, :width], gate_proj[...], 1, 0)
-    loads[2].wait()
     up_value = contract(landed[:, :width], up_proj[...], 1, 0)
     sigmoid = 1.0 / (1.0 + jnp.exp(-gate_value))
     silu = gate_value * sigmoid
     hidden = (silu * up_value).astype(BF16)
-    loads[3].wait()
-    loads[4].wait()
     hidden_grad = contract(landed[:, width:], down_proj[...], 1, 1)
     slope = up_value * sigmoid * (1.0 + gate_value * (1.0 - sigmoid))
     pair_grad[:, :hid] = (hidden_grad * slope).astype(BF16)
@@ -175,16 +160,11 @@
         (shape(data_count, width // data_count, 3 * hid), shape(count, 2 * hid)),
         landed, gate_proj[0], up_proj[0], down_proj[0],
         flops=6 * dot_flops,
-        vmem=ALONE,
-        in_specs=[far] * 4,
+        vmem=BESIDE,
+        in_specs=[here] * 4,
         out_specs=[far, here],
         scratch_shapes=[
-            pltpu.VMEM((count, 2 * width), BF16),
-            pltpu.VMEM((width, hid), BF16),
-            pltpu.VMEM((width, hid), BF16),
-            pltpu.VMEM((hid, width), BF16),
             pltpu.VMEM((data_count, width // data_count, 3 * hid), BF16),
-            pltpu.SemaphoreType.DMA((5,)),
             pltpu.SemaphoreType.DMA((data_count,)),
         ],
     )

time: 189 us -> 187 us (0.989)
  Pallas kernels: 13.3 us -> 10.4 us
  waiting for transfers between devices: 2.45 us -> 4.35 us
    pallas_call x5, Pallas kernels: 13.3 us -> 10.4 us  [run(): pl.pallas_call(kernel, out_shape=out, cost_estimate=pl.CostEstimate(flops...]
    reduce_scatter x1, waiting for transfers between devices: 2.44 us -> 4.33 us  [shards(): lax.psum_scatter(partial.reshape(width, 3 * hid), 'dp', scatter_dimension...]
where the time goes in v4:
time: 187 us; the launch traced here: 186 us
  blocking collectives  156 us (83%)
  between operations  14.1 us (8%)
  Pallas kernels  10.4 us (6%)
  waiting for transfers between devices  4.35 us (2%)
    all_to_all x4, blocking collectives, over(): return lax.all_to_all(blocks, axis, split_axis=0, concat_axis=0, tiled=True)  156 us
    pallas_call x5, Pallas kernels, run(): pl.pallas_call(kernel, out_shape=out, cost_estimate=pl.CostEstimate(flops...  10.4 us
    reduce_scatter x1, waiting for transfers between devices, shards(): lax.psum_scatter(partial.reshape(width, 3 * hid), 'dp', scatter_dimension...  4.33 us
  transfers between devices with their start and end apart: 1, of which 1 were waited for; matrix products, arithmetic and copies ran while one was open for 1% of the time, Pallas kernels for 1%

profile of v4, /device:TPU:1, one launch (start us, length us, event | category | flops | bytes accessed | tf_op | source)
XLA Modules:
  0.0 186.2 jit_solution(11849482606856997172)
XLA Ops:
  7.2 0.0 reduce-scatter.2.cloned.1.call-start
  7.2 2.0 %shard_map.111 = bf16[8,16,4224]{2,1,0:T(8,128)(2,1)} custom-call(bf16[16,2048]{1,0:T(8,128)(2,1)} %tokens.1, bf16[16,2048]{1,0:T(8,128)(2,1)} %cotangent.1, s32[8,16]{1,0:T(8,128)} %bitcast.23, s32[4,16]{1,0:T(4,128)} %bitcast.24, bf16[8,16]{1,0:T(8,128)(2,1)} %bitcast.25), custom_call_target="tpu_custom_call" | custom-call | bytes 1213440 | tf_op jit(solution)/shard_map/pallas_call | solution.py:115
  9.2 25.3 %all_to_all.20.arrived = bf16[8,16,4224]{2,1,0:T(8,128)(2,1)S(1)} all-to-all(bf16[8,16,4224]{2,1,0:T(8,128)(2,1)} %shard_map.111), channel_id=1, replica_groups=mesh['dp'=8,'group'=8,'node'=16] {'group'}, dimensions={0} | all-to-all | bytes 2162688 | tf_op jit(solution)/shard_map/all_to_all | solution.py:140
  34.5 0.0 copy-start.4
  34.5 0.9 shard_map.112
  35.4 0.0 copy-start.2
  35.4 0.0 copy-start
  35.4 0.0 copy-start.1
  35.4 80.2 %all_to_all.21 = bf16[16,16,4096]{2,1,0:T(8,128)(2,1)S(1)} all-to-all(bf16[16,16,4096]{2,1,0:T(8,128)(2,1)S(1)} %get-tuple-element.12), channel_id=1, replica_groups=mesh['dp'=8,'group'=8,'node'=16] {'node'}, dimensions={0} | all-to-all | bytes 4194304 | tf_op jit(solution)/shard_map/all_to_all | solution.py:140
  115.6 0.0 copy-done.2
  115.6 0.0 copy-done.4
  115.6 0.0 copy-done
  115.6 0.0 copy-done.1
  115.6 4.4 %shard_map.113 = (bf16[8,256,1152]{2,1,0:T(8,128)(2,1)}, bf16[256,768]{1,0:T(8,128)(2,1)S(1)}) custom-call(bf16[256,4096]{1,0:T(8,128)(2,1)S(1)} %bitcast.14, bf16[2048,384]{1,0:T(8,128)(2,1)S(1)} %bitcast.15, bf16[2048,384]{1,0:T(8,128)(2,1)S(1)} %bitcast.17, bf16[384,2048]{1,0:T(8,128)(2,1)S(1)} %bitcast.19), custom_call_target="tpu_custom_call" | custom-call | flops 2415919104 | bytes 11927552 | tf_op jit(solution)/shard_map/pallas_call | solution.py:115
  120.0 0.0 reduce-scatter.2.cloned.1.call-update
  120.0 1.3 shard_map.114
  121.3 0.0 copy-start.3
  121.3 31.4 %all_to_all.22 = bf16[16,16,2048]{2,1,0:T(8,128)(2,1)S(1)} all-to-all(bf16[16,16,2048]{2,1,0:T(8,128)(2,1)S(1)} %bitcast.13), channel_id=1, replica_groups=mesh['dp'=8,'group'=8,'node'=16] {'node'}, dimensions={0} | all-to-all | bytes 2097152 | tf_op jit(solution)/shard_map/all_to_all | solution.py:140
  152.7 0.0 copy-done.3
  152.7 0.3 convolution_convert_fusion
  153.0 19.4 %all_to_all.23 = bf16[8,16,2048]{2,1,0:T(8,128)(2,1)S(1)} all-to-all(bf16[8,16,2048]{2,1,0:T(8,128)(2,1)S(1)} %bitcast.22), channel_id=1, replica_groups=mesh['dp'=8,'group'=8,'node'=16] {'group'}, dimensions={0} | all-to-all | bytes 1048576 | tf_op jit(solution)/shard_map/all_to_all | solution.py:140
  172.5 0.7 reduce_sum.12
  173.2 4.3 %reduce-scatter.2.cloned.1.call-done.total = bf16[256,1152]{1,0:T(8,128)(2,1)} async-done(((bf16[2048,1152]{1,0:T(8,128)(2,1)}), bf16[256,1152]{1,0:T(8,128)(2,1)}) %reduce-scatter.2.cloned.1.call-update) | async-done | bytes 589840 | tf_op jit(solution)/shard_map/reduce_scatter | solution.py:171
  177.5 1.9 %shard_map.115 = (bf16[1,256,384]{2,1,0:T(8,128)(2,1)}, bf16[1,256,384]{2,1,0:T(8,128)(2,1)}, bf16[1,384,256]{2,1,0:T(8,128)(2,1)}) custom-call(bf16[256,1152]{1,0:T(8,128)(2,1)} %reduce-scatter.2.cloned.1.call-done.total), custom_call_target="tpu_custom_call" | custom-call | bytes 1179648 | tf_op jit(solution)/shard_map/pallas_call | solution.py:115
Async XLA Ops:
  7.2 170.3 %reduce-scatter.2.cloned.1.call-start = ((), (), s32[]{:S(2)}) async-start(), calls=%async_computation.5 | async-start | bytes 5308416 | tf_op jit(solution)/shard_map/reduce_scatter | solution.py:171
  34.5 81.1 %copy-start.4 = (bf16[1,384,2048]{2,1,0:T(8,128)(2,1)S(1)}, bf16[1,384,2048]{2,1,0:T(8,128)(2,1)}, u32[]{:S(2)}) copy-start(bf16[1,384,2048]{2,1,0:T(8,128)(2,1)} %param.15) | copy-start | bytes 4718596
  35.4 80.2 %copy-start.2 = (bf16[256,128]{1,0:T(8,128)(2,1)}, bf16[256,128]{1,0:T(8,128)(2,1)S(1)}, u32[]{:S(2)}) copy-start(bf16[256,128]{1,0:T(8,128)(2,1)S(1)} %get-tuple-element.11) | copy-start | bytes 196612
  35.4 80.2 %copy-start = (bf16[1,2048,384]{2,1,0:T(8,128)(2,1)S(1)}, bf16[1,2048,384]{2,1,0:T(8,128)(2,1)}, u32[]{:S(2)}) copy-start(bf16[1,2048,384]{2,1,0:T(8,128)(2,1)} %param.13) | copy-start | bytes 4718596
  35.4 80.2 %copy-start.1 = (bf16[1,2048,384]{2,1,0:T(8,128)(2,1)S(1)}, bf16[1,2048,384]{2,1,0:T(8,128)(2,1)}, u32[]{:S(2)}) copy-start(bf16[1,2048,384]{2,1,0:T(8,128)(2,1)} %param.14) | copy-start | bytes 4718596
  121.3 31.4 %copy-start.3 = (bf16[256,128]{1,0:T(8,128)(2,1)S(1)}, bf16[256,128]{1,0:T(8,128)(2,1)}, u32[]{:S(2)}) copy-start(bf16[256,128]{1,0:T(8,128)(2,1)} %copy-done.2) | copy-start | bytes 196612
Sparse Core Ops, SparseCore 0:
  120.1 57.3 reduce-scatter.1

commit v5 on v4

--- a/solution.py
+++ b/solution.py
@@ -178,8 +178,19 @@
     home = over("group", group_grad.reshape(group_count, tok_count, width))
     grad_tokens = jnp.sum(home.astype(F32), axis=0).astype(BF16)
     cut = width // data_count
+    step = cut // 2
     gate_out, up_out, down_out = run(
-        split_kernel, (shape(1, cut, hid), shape(1, cut, hid), shape(1, hid, cut)), total, vmem=ALONE
+        split_kernel,
+        (shape(1, cut, hid), shape(1, cut, hid), shape(1, hid, cut)),
+        total,
+        vmem=ALONE,
+        grid=(2,),
+        in_specs=[pl.BlockSpec((step, 3 * hid), lambda i: (i, 0))],
+        out_specs=[
+            pl.BlockSpec((1, step, hid), lambda i: (0, i, 0)),
+            pl.BlockSpec((1, step, hid), lambda i: (0, i, 0)),
+            pl.BlockSpec((1, hid, step), lambda i: (0, 0, i)),
+        ],
     )
     return grad_tokens, gate_out, up_out, down_out
 

time: 187 us -> 186 us (level)
  no operation moved by 1% of the time
where the time goes in v5:
time: 186 us
  blocking collectives  156 us (84%)
  between operations  14.1 us (8%)
  Pallas kernels  10.3 us (6%)
  waiting for transfers between devices  4.35 us (2%)
    all_to_all x4, blocking collectives, over(): return lax.all_to_all(blocks, axis, split_axis=0, concat_axis=0, tiled=True)  156 us
    pallas_call x5, Pallas kernels, run(): pl.pallas_call(kernel, out_shape=out, cost_estimate=pl.CostEstimate(flops...  10.3 us
    reduce_scatter x1, waiting for transfers between devices, shards(): lax.psum_scatter(partial.reshape(width, 3 * hid), 'dp', scatter_dimension...  4.33 us
  transfers between devices with their start and end apart: 1, of which 1 were waited for; matrix products, arithmetic and copies ran while one was open for 1% of the time, Pallas kernels for 1%

profile of v5, /device:TPU:1, one launch (start us, length us, event | category | flops | bytes accessed | tf_op | source)
XLA Modules:
  0.0 186.1 jit_solution(12420551486374508016)
XLA Ops:
  7.2 0.0 reduce-scatter.2.cloned.1.call-start
  7.2 2.0 %shard_map.111 = bf16[8,16,4224]{2,1,0:T(8,128)(2,1)} custom-call(bf16[16,2048]{1,0:T(8,128)(2,1)} %tokens.1, bf16[16,2048]{1,0:T(8,128)(2,1)} %cotangent.1, s32[8,16]{1,0:T(8,128)} %bitcast.23, s32[4,16]{1,0:T(4,128)} %bitcast.24, bf16[8,16]{1,0:T(8,128)(2,1)} %bitcast.25), custom_call_target="tpu_custom_call" | custom-call | bytes 1213440 | tf_op jit(solution)/shard_map/pallas_call | solution.py:115
  9.2 25.3 %all_to_all.20.arrived = bf16[8,16,4224]{2,1,0:T(8,128)(2,1)S(1)} all-to-all(bf16[8,16,4224]{2,1,0:T(8,128)(2,1)} %shard_map.111), channel_id=1, replica_groups=mesh['dp'=8,'group'=8,'node'=16] {'group'}, dimensions={0} | all-to-all | bytes 2162688 | tf_op jit(solution)/shard_map/all_to_all | solution.py:140
  34.5 0.0 copy-start.4
  34.5 0.9 shard_map.112
  35.4 0.0 copy-start.2
  35.4 0.0 copy-start
  35.4 0.0 copy-start.1
  35.4 80.2 %all_to_all.21 = bf16[16,16,4096]{2,1,0:T(8,128)(2,1)S(1)} all-to-all(bf16[16,16,4096]{2,1,0:T(8,128)(2,1)S(1)} %get-tuple-element.12), channel_id=1, replica_groups=mesh['dp'=8,'group'=8,'node'=16] {'node'}, dimensions={0} | all-to-all | bytes 4194304 | tf_op jit(solution)/shard_map/all_to_all | solution.py:140
  115.6 0.0 copy-done.2
  115.6 0.0 copy-done.4
  115.6 0.0 copy-done
  115.6 0.0 copy-done.1
  115.6 4.4 %shard_map.113 = (bf16[8,256,1152]{2,1,0:T(8,128)(2,1)}, bf16[256,768]{1,0:T(8,128)(2,1)S(1)}) custom-call(bf16[256,4096]{1,0:T(8,128)(2,1)S(1)} %bitcast.14, bf16[2048,384]{1,0:T(8,128)(2,1)S(1)} %bitcast.15, bf16[2048,384]{1,0:T(8,128)(2,1)S(1)} %bitcast.17, bf16[384,2048]{1,0:T(8,128)(2,1)S(1)} %bitcast.19), custom_call_target="tpu_custom_call" | custom-call | flops 2415919104 | bytes 11927552 | tf_op jit(solution)/shard_map/pallas_call | solution.py:115
  120.0 0.0 reduce-scatter.2.cloned.1.call-update
  120.0 1.3 shard_map.114
  121.3 0.0 copy-start.3
  121.3 31.4 %all_to_all.22 = bf16[16,16,2048]{2,1,0:T(8,128)(2,1)S(1)} all-to-all(bf16[16,16,2048]{2,1,0:T(8,128)(2,1)S(1)} %bitcast.13), channel_id=1, replica_groups=mesh['dp'=8,'group'=8,'node'=16] {'node'}, dimensions={0} | all-to-all | bytes 2097152 | tf_op jit(solution)/shard_map/all_to_all | solution.py:140
  152.7 0.0 copy-done.3
  152.7 0.3 convolution_convert_fusion
  153.0 19.4 %all_to_all.23 = bf16[8,16,2048]{2,1,0:T(8,128)(2,1)S(1)} all-to-all(bf16[8,16,2048]{2,1,0:T(8,128)(2,1)S(1)} %bitcast.22), channel_id=1, replica_groups=mesh['dp'=8,'group'=8,'node'=16] {'group'}, dimensions={0} | all-to-all | bytes 1048576 | tf_op jit(solution)/shard_map/all_to_all | solution.py:140
  172.5 0.7 reduce_sum.12
  173.2 4.3 %reduce-scatter.2.cloned.1.call-done.total = bf16[256,1152]{1,0:T(8,128)(2,1)} async-done(((bf16[2048,1152]{1,0:T(8,128)(2,1)}), bf16[256,1152]{1,0:T(8,128)(2,1)}) %reduce-scatter.2.cloned.1.call-update) | async-done | bytes 589840 | tf_op jit(solution)/shard_map/reduce_scatter | solution.py:171
  177.5 1.8 shard_map.115
Async XLA Ops:
  7.2 170.3 %reduce-scatter.2.cloned.1.call-start = ((), (), s32[]{:S(2)}) async-start(), calls=%async_computation.5 | async-start | bytes 5308416 | tf_op jit(solution)/shard_map/reduce_scatter | solution.py:171
  34.5 81.1 %copy-start.4 = (bf16[1,384,2048]{2,1,0:T(8,128)(2,1)S(1)}, bf16[1,384,2048]{2,1,0:T(8,128)(2,1)}, u32[]{:S(2)}) copy-start(bf16[1,384,2048]{2,1,0:T(8,128)(2,1)} %param.15) | copy-start | bytes 4718596
  35.4 80.2 %copy-start.2 = (bf16[256,128]{1,0:T(8,128)(2,1)}, bf16[256,128]{1,0:T(8,128)(2,1)S(1)}, u32[]{:S(2)}) copy-start(bf16[256,128]{1,0:T(8,128)(2,1)S(1)} %get-tuple-element.11) | copy-start | bytes 196612
  35.4 80.2 %copy-start = (bf16[1,2048,384]{2,1,0:T(8,128)(2,1)S(1)}, bf16[1,2048,384]{2,1,0:T(8,128)(2,1)}, u32[]{:S(2)}) copy-start(bf16[1,2048,384]{2,1,0:T(8,128)(2,1)} %param.13) | copy-start | bytes 4718596
  35.4 80.2 %copy-start.1 = (bf16[1,2048,384]{2,1,0:T(8,128)(2,1)S(1)}, bf16[1,2048,384]{2,1,0:T(8,128)(2,1)}, u32[]{:S(2)}) copy-start(bf16[1,2048,384]{2,1,0:T(8,128)(2,1)} %param.14) | copy-start | bytes 4718596
  121.3 31.4 %copy-start.3 = (bf16[256,128]{1,0:T(8,128)(2,1)S(1)}, bf16[256,128]{1,0:T(8,128)(2,1)}, u32[]{:S(2)}) copy-start(bf16[256,128]{1,0:T(8,128)(2,1)} %copy-done.2) | copy-start | bytes 196612
Sparse Core Ops, SparseCore 0:
  120.1 57.3 reduce-scatter.1
